TPU v7x, 512 devices: a whole 4x8x8 slice. The times are simulated.
512 devices in a mesh: gx: 16 (over y, core), gy: 32 (over z, x).
Axes of the slice: x: 4, y: 8, z: 8, core: 2. Of those that a mesh axis runs over, the one named last changes fastest.
Arguments:
- misfit: float32 [384, 768, 128], P('gx', 'gy'), may hold values from -6 to 6
- bleach_mask: int32 [384, 768, 128], P('gx', 'gy'), may hold values 0 or 1
- labels: int32 [384, 768, 128], P('gx', 'gy'), may hold values from 0 to 2
- diffusion: float32 [384, 768, 128], P('gx', 'gy'), may hold values from 0.01 to 0.08
- bind_table: float32 [3], replicated, may hold values from 0.05 to 0.4
- release_table: float32 [3], replicated, may hold values from 0.05 to 0.4
- kern_x: float32 [31], replicated, may hold values from 0.1 to 0.3
- kern_y: float32 [31], replicated, may hold values from 0.1 to 0.3
- kern_z: float32 [63], replicated, may hold values from 0.05 to 0.2
- free_states: bfloat16 [2, 384, 768, 128], P(None, 'gx', 'gy'), may hold values from 0 to 2
Outputs:
- diff_grad: float32 [384, 768, 128], P('gx', 'gy')
- adjoint_initial: float32 [2, 384, 768, 128], P(None, 'gx', 'gy')
All inputs are finite; a program needn't handle non-finite values. No bound on the sum of `bleach_mask` on one device may be relied on, other than what follows from the above.
Results may differ from a plain program's by a relative error of at most 0.0003.
Values may be sent and summed in bfloat16 or wider, within the bound.
No kernel may reach another device: no remote copies, remote signals or barrier semaphores. Data moves between devices by JAX's collectives and lax.ppermute only.
A program may use at most 64 MiB of HBM per device.

v0:
```python
import jax
import jax.numpy as jnp
from jax import lax
from jax.sharding import PartitionSpec as P


def padded(x, sides, width):
    for axis, dim in sides:
        size, length = (lax.axis_size(axis), x.shape[dim])
        up = [(i, (i + 1) % size) for i in range(size - 1)]
        down = [(j, i) for i, j in up]
        last = lax.slice_in_dim(x, length - width, length, axis=dim)
        first = lax.slice_in_dim(x, 0, width, axis=dim)
        before = lax.ppermute(last, axis, up)
        after = lax.ppermute(first, axis, down)
        x = jnp.concatenate([before, x, after], axis=dim)
    return x


def band_matrix(kern, rows, cols, offset_base):
    span = kern.shape[0]
    row_index = jnp.arange(rows, dtype=jnp.int32)[:, None]
    col_index = jnp.arange(cols, dtype=jnp.int32)[None, :]
    offset = col_index - row_index + offset_base
    taps = jnp.arange(span, dtype=jnp.int32)
    hit = offset[:, :, None] == taps[None, None, :]
    return jnp.sum(jnp.where(hit, kern[None, None, :], jnp.zeros((), jnp.float32)), axis=2)


def neighbour_list(extended):
    center = extended[1:-1, 1:-1]
    zero_plane = jnp.zeros_like(center[:, :, :1])
    return [
        extended[2:, 1:-1],
        extended[:-2, 1:-1],
        extended[1:-1, 2:],
        extended[1:-1, :-2],
        jnp.concatenate([center[:, :, 1:], zero_plane], axis=2),
        jnp.concatenate([zero_plane, center[:, :, :-1]], axis=2),
    ]


def shards(
    misfit,
    bleach_mask,
    labels,
    diffusion,
    bind_table,
    release_table,
    kern_x,
    kern_y,
    kern_z,
    free_states,
):
    highest = lax.Precision.HIGHEST
    rows_x, rows_y, depth = misfit.shape
    steps_count = free_states.shape[0]
    blur_reach = (kern_x.shape[0] - 1) // 2
    reach_depth = (kern_z.shape[0] - 1) // 2
    margin_extra = 0
    rim_width = blur_reach + margin_extra
    out_x = rows_x + 2 * margin_extra
    out_y = rows_y + 2 * margin_extra
    zmatrix = band_matrix(kern_z, depth, depth, reach_depth)
    weighted = (1.0 + 3.0 * bleach_mask.astype(jnp.float32)) * misfit
    xmatrix = band_matrix(kern_x, out_x, out_x + 2 * blur_reach, 0)
    ymatrix = band_matrix(kern_y, out_y, out_y + 2 * blur_reach, 0)
    extended = padded(weighted, (("gx", 0), ("gy", 1)), rim_width)
    partial_blur = jnp.einsum("ie,eyz->iyz", xmatrix, extended, precision=highest)
    blurred = jnp.einsum("je,iez->ijz", ymatrix, partial_blur, precision=highest)
    image_adjoint = jnp.einsum("xyz,wz->xyw", blurred, zmatrix, precision=highest)
    bind = jnp.zeros_like(diffusion)
    release = jnp.zeros_like(diffusion)
    for kind in range(bind_table.shape[0]):
        hit = labels == kind
        bind = jnp.where(hit, bind_table[kind], bind)
        release = jnp.where(hit, release_table[kind], release)
    coeff_ext = padded(diffusion, (("gx", 0), ("gy", 1)), 1)
    couplings = []
    slopes = []
    for other in neighbour_list(coeff_ext):
        total = diffusion + other
        couplings.append(2.0 * diffusion * other / total)
        slopes.append(2.0 * other * other / (total * total))
    states_ext = padded(free_states, (("gx", 1), ("gy", 2)), 1)
    adj_free = image_adjoint
    adj_bound = 0.5 * image_adjoint
    diff_grad = jnp.zeros_like(diffusion)
    for step in reversed(range(steps_count)):
        state_ext = states_ext[step].astype(jnp.float32)
        state = state_ext[1:-1, 1:-1]
        adj_ext = padded(adj_free, (("gx", 0), ("gy", 1)), 1)
        spread = jnp.zeros_like(diffusion)
        for coupling, slope, state_other, adj_other in zip(
            couplings, slopes, neighbour_list(state_ext), neighbour_list(adj_ext)
        ):
            change = adj_other - adj_free
            spread = spread + coupling * change
            diff_grad = diff_grad - slope * (state_other - state) * change
        new_free = adj_free + spread - bind * adj_free + bind * adj_bound
        adj_bound = adj_bound + release * adj_free - release * adj_bound
        adj_free = new_free
    return (diff_grad, jnp.stack([adj_free, adj_bound]))


def solution(mesh):
    in_specs = (
        P("gx", "gy", None),
        P("gx", "gy", None),
        P("gx", "gy", None),
        P("gx", "gy", None),
        P(),
        P(),
        P(),
        P(),
        P(),
        P(None, "gx", "gy", None),
    )
    out_specs = (P("gx", "gy", None), P(None, "gx", "gy", None))
    return jax.shard_map(shards, mesh=mesh, in_specs=in_specs, out_specs=out_specs, check_vma=False)
```

profile of v0, /device:TPU:288, one launch (start us, length us, event | category | flops | bytes accessed | tf_op | source)
XLA Modules:
  0.0 113.0 jit_solution(13056518347386370698)
XLA Ops:
  0.6 0.0 copy-start
  0.7 0.9 fusion.71
  1.6 1.9 %collective-permute-start.1 = (bf16[2,1,24,128]{3,2,1,0:T(8,128)(2,1)S(1)}, bf16[2,1,24,128]{3,2,1,0:T(8,128)(2,1)S(1)}, u32[]{:S(2)}, u32[]{:S(2)}) collective-permute-start(bf16[2,1,24,128]{3,2,1,0:T(8,128)(2,1)S(1)} %get-tuple-element.40), channel_id=1, source_target_pairs={{0,32},{32,64},{64,96},{96,128},{128,160},{160,192},{192,224},{224... | collective-permute-start | bytes 36872 | tf_op jit(solution)/shard_map/ppermute | solution.py:14
  3.5 4.9 %collective-permute-start.2 = (bf16[2,1,24,128]{3,2,1,0:T(8,128)(2,1)S(1)}, bf16[2,1,24,128]{3,2,1,0:T(8,128)(2,1)S(1)}, u32[]{:S(2)}, u32[]{:S(2)}) collective-permute-start(bf16[2,1,24,128]{3,2,1,0:T(8,128)(2,1)S(1)} %get-tuple-element.39), channel_id=1, source_target_pairs={{32,0},{64,32},{96,64},{128,96},{160,128},{192,160},{224,192},{256... | collective-permute-start | bytes 36872 | tf_op jit(solution)/shard_map/ppermute | solution.py:15
  8.3 0.7 fusion.70
  9.1 1.9 %collective-permute-start.10 = (f32[1,24,128]{2,1,0:T(8,128)S(1)}, f32[1,24,128]{2,1,0:T(8,128)S(1)}, u32[]{:S(2)}, u32[]{:S(2)}) collective-permute-start(f32[1,24,128]{2,1,0:T(8,128)S(1)} %get-tuple-element.38), channel_id=1, source_target_pairs={{0,32},{32,64},{64,96},{96,128},{128,160},{160,192},{192,224},{224... | collective-permute-start | bytes 36872 | tf_op jit(solution)/shard_map/ppermute | solution.py:14
  11.0 4.9 %collective-permute-start = (f32[1,24,128]{2,1,0:T(8,128)S(1)}, f32[1,24,128]{2,1,0:T(8,128)S(1)}, u32[]{:S(2)}, u32[]{:S(2)}) collective-permute-start(f32[1,24,128]{2,1,0:T(8,128)S(1)} %get-tuple-element.37), channel_id=1, source_target_pairs={{32,0},{64,32},{96,64},{128,96},{160,128},{192,160},{224,192},{256... | collective-permute-start | bytes 36872 | tf_op jit(solution)/shard_map/ppermute | solution.py:15
  15.8 1.1 add_multiply_fusion
  17.0 1.9 %collective-permute-start.6 = (f32[15,24,128]{2,1,0:T(8,128)S(1)}, f32[15,24,128]{2,1,0:T(8,128)S(1)}, u32[]{:S(2)}, u32[]{:S(2)}) collective-permute-start(f32[15,24,128]{2,1,0:T(8,128)S(1)} %get-tuple-element.36), channel_id=1, source_target_pairs={{32,0},{64,32},{96,64},{128,96},{160,128},{192,160},{224,192},{256... | collective-permute-start | bytes 552968 | tf_op jit(solution)/shard_map/ppermute | solution.py:15
  18.9 0.7 fusion.73
  19.6 0.5 select_reduce_fusion
  20.1 0.2 select_reduce_fusion.1
  20.3 0.6 fusion.72
  20.9 2.4 %collective-permute-start.5 = (f32[15,24,128]{2,1,0:T(8,128)S(1)}, f32[15,24,128]{2,1,0:T(8,128)S(1)}, u32[]{:S(2)}, u32[]{:S(2)}) collective-permute-start(f32[15,24,128]{2,1,0:T(8,128)S(1)} %get-tuple-element.35), channel_id=1, source_target_pairs={{0,32},{32,64},{64,96},{96,128},{128,160},{160,192},{192,224},{224... | collective-permute-start | bytes 552968 | tf_op jit(solution)/shard_map/ppermute | solution.py:14
  23.3 0.1 constant_dynamic-update-slice_fusion.1
  23.5 3.8 %collective-permute-start.4 = (bf16[2,26,1,128]{3,2,1,0:T(2,128)(2,1)S(1)}, bf16[2,26,1,128]{3,2,1,0:T(2,128)(2,1)S(1)}, u32[]{:S(2)}, u32[]{:S(2)}) collective-permute-start(bf16[2,26,1,128]{3,2,1,0:T(2,128)(2,1)S(1)} %get-tuple-element.24), channel_id=1, source_target_pairs={{1,0},{2,1},{3,2},{4,3},{5,4},{6,5},{7,6},{8,7},{9,8},{10,9},{11,1... | collective-permute-start | bytes 39944 | tf_op jit(solution)/shard_map/ppermute | solution.py:15
  27.2 2.1 %collective-permute-start.3 = (bf16[2,26,1,128]{3,2,1,0:T(2,128)(2,1)S(1)}, bf16[2,26,1,128]{3,2,1,0:T(2,128)(2,1)S(1)}, u32[]{:S(2)}, u32[]{:S(2)}) collective-permute-start(bf16[2,26,1,128]{3,2,1,0:T(2,128)(2,1)S(1)} %get-tuple-element.23), channel_id=1, source_target_pairs={{0,1},{1,2},{2,3},{3,4},{4,5},{5,6},{6,7},{7,8},{8,9},{9,10},{10,1... | collective-permute-start | bytes 39944 | tf_op jit(solution)/shard_map/ppermute | solution.py:14
  29.5 0.1 fusion.59
  29.5 7.1 %collective-permute-start.8 = (f32[54,15,128]{2,1,0:T(8,128)S(1)}, f32[54,15,128]{2,1,0:T(8,128)S(1)}, u32[]{:S(2)}, u32[]{:S(2)}) collective-permute-start(f32[54,15,128]{2,1,0:T(8,128)S(1)} %get-tuple-element.10), channel_id=1, source_target_pairs={{1,0},{2,1},{3,2},{4,3},{5,4},{6,5},{7,6},{8,7},{9,8},{10,9},{11,1... | collective-permute-start | bytes 1244168 | tf_op jit(solution)/shard_map/ppermute | solution.py:15
  36.6 1.9 %collective-permute-start.7 = (f32[54,15,128]{2,1,0:T(8,128)S(1)}, f32[54,15,128]{2,1,0:T(8,128)S(1)}, u32[]{:S(2)}, u32[]{:S(2)}) collective-permute-start(f32[54,15,128]{2,1,0:T(8,128)S(1)} %get-tuple-element.9), channel_id=1, source_target_pairs={{0,1},{1,2},{2,3},{3,4},{4,5},{5,6},{6,7},{7,8},{8,9},{9,10},{10,1... | collective-permute-start | bytes 1244168 | tf_op jit(solution)/shard_map/ppermute | solution.py:14
  38.6 1.9 %collective-permute-start.14 = (f32[26,1,128]{2,1,0:T(1,128)S(1)}, f32[26,1,128]{2,1,0:T(1,128)S(1)}, u32[]{:S(2)}, u32[]{:S(2)}) collective-permute-start(f32[26,1,128]{2,1,0:T(1,128)S(1)} %get-tuple-element.20), channel_id=1, source_target_pairs={{0,1},{1,2},{2,3},{3,4},{4,5},{5,6},{6,7},{7,8},{8,9},{9,10},{10,1... | collective-permute-start | bytes 39944 | tf_op jit(solution)/shard_map/ppermute | solution.py:14
  40.5 7.2 %collective-permute-start.12 = (f32[26,1,128]{2,1,0:T(1,128)S(1)}, f32[26,1,128]{2,1,0:T(1,128)S(1)}, u32[]{:S(2)}, u32[]{:S(2)}) collective-permute-start(f32[26,1,128]{2,1,0:T(1,128)S(1)} %get-tuple-element.19), channel_id=1, source_target_pairs={{1,0},{2,1},{3,2},{4,3},{5,4},{6,5},{7,6},{8,7},{9,8},{10,9},{11,1... | collective-permute-start | bytes 39944 | tf_op jit(solution)/shard_map/ppermute | solution.py:15
  47.8 0.2 pad_maximum_fusion.3
  48.0 5.2 %collective-permute-done.7 = f32[54,15,128]{2,1,0:T(8,128)S(1)} collective-permute-done((f32[54,15,128]{2,1,0:T(8,128)S(1)}, f32[54,15,128]{2,1,0:T(8,128)S(1)}, u32[]{:S(2)}, u32[]{:S(2)}) %collective-permute-start.7) | collective-permute-done | bytes 414752 | tf_op jit(solution)/shard_map/ppermute | solution.py:14
  53.2 0.2 pad_maximum_fusion
  53.4 1.0 fusion
  54.4 0.6 convolution_bitcast_fusion
  55.0 0.4 fusion.55
  55.4 3.0 %collective-permute-start.9 = (f32[1,24,128]{2,1,0:T(8,128)S(1)}, f32[1,24,128]{2,1,0:T(8,128)S(1)}, u32[]{:S(2)}, u32[]{:S(2)}) collective-permute-start(f32[1,24,128]{2,1,0:T(8,128)S(1)} %get-tuple-element.30), channel_id=1, source_target_pairs={{32,0},{64,32},{96,64},{128,96},{160,128},{192,160},{224,192},{256... | collective-permute-start | bytes 36872 | tf_op jit(solution)/shard_map/ppermute | solution.py:15
  58.5 1.9 %collective-permute-start.11 = (f32[1,24,128]{2,1,0:T(8,128)S(1)}, f32[1,24,128]{2,1,0:T(8,128)S(1)}, u32[]{:S(2)}, u32[]{:S(2)}) collective-permute-start(f32[1,24,128]{2,1,0:T(8,128)S(1)} %get-tuple-element.29), channel_id=1, source_target_pairs={{0,32},{32,64},{64,96},{96,128},{128,160},{160,192},{192,224},{224... | collective-permute-start | bytes 36872 | tf_op jit(solution)/shard_map/ppermute | solution.py:14
  60.4 0.1 fusion.52
  60.5 4.2 %collective-permute-done.11 = f32[1,24,128]{2,1,0:T(8,128)S(1)} collective-permute-done((f32[1,24,128]{2,1,0:T(8,128)S(1)}, f32[1,24,128]{2,1,0:T(8,128)S(1)}, u32[]{:S(2)}, u32[]{:S(2)}) %collective-permute-start.11) | collective-permute-done | bytes 12320 | tf_op jit(solution)/shard_map/ppermute | solution.py:14
  64.7 1.9 %collective-permute-start.15 = (f32[26,1,128]{2,1,0:T(1,128)S(1)}, f32[26,1,128]{2,1,0:T(1,128)S(1)}, u32[]{:S(2)}, u32[]{:S(2)}) collective-permute-start(f32[26,1,128]{2,1,0:T(1,128)S(1)} %get-tuple-element.22), channel_id=1, source_target_pairs={{0,1},{1,2},{2,3},{3,4},{4,5},{5,6},{6,7},{7,8},{8,9},{9,10},{10,1... | collective-permute-start | bytes 39944 | tf_op jit(solution)/shard_map/ppermute | solution.py:14
  66.7 7.2 %collective-permute-start.13 = (f32[26,1,128]{2,1,0:T(1,128)S(1)}, f32[26,1,128]{2,1,0:T(1,128)S(1)}, u32[]{:S(2)}, u32[]{:S(2)}) collective-permute-start(f32[26,1,128]{2,1,0:T(1,128)S(1)} %get-tuple-element.21), channel_id=1, source_target_pairs={{1,0},{2,1},{3,2},{4,3},{5,4},{6,5},{7,6},{8,7},{9,8},{10,9},{11,1... | collective-permute-start | bytes 39944 | tf_op jit(solution)/shard_map/ppermute | solution.py:15
  73.9 0.2 fusion.67
  74.2 1.1 %collective-permute-done.13 = f32[26,1,128]{2,1,0:T(1,128)S(1)} collective-permute-done((f32[26,1,128]{2,1,0:T(1,128)S(1)}, f32[26,1,128]{2,1,0:T(1,128)S(1)}, u32[]{:S(2)}, u32[]{:S(2)}) %collective-permute-start.13) | collective-permute-done | bytes 13344 | tf_op jit(solution)/shard_map/ppermute | solution.py:15
  75.3 4.7 %subtract_bitcast_fusion = (f32[1,24,24,128]{3,2,1,0:T(8,128)S(1)}, f32[24,24,128]{2,1,0:T(8,128)S(1)}, pred[24,24,128]{2,1,0:T(8,128)(4,1)S(1)}, pred[24,24,128]{2,1,0:T(8,128)(4,1)S(1)}, pred[24,24,128]{2,1,0:T(8,128)(4,1)S(1)}) fusion(f32[24,24,128]{2,1,0:T(8,128)S(1)} %fusion.55, f32[]{:T(128)} %bitcast.13, f32[]{:T(128)} %bitcast.12, f32[]{:T(128)} %bitcast.11, ...), kind=kLoop, calls=%fused_computation.95 | loop fusion | flops 5234688 | bytes 3288088 | tf_op jit(solution)/shard_map/stack | solution.py:103
  80.0 1.9 %collective-permute-start.16 = (f32[1,24,128]{2,1,0:T(8,128)S(1)}, f32[1,24,128]{2,1,0:T(8,128)S(1)}, u32[]{:S(2)}, u32[]{:S(2)}) collective-permute-start(f32[1,24,128]{2,1,0:T(8,128)S(1)} %get-tuple-element.26), channel_id=1, source_target_pairs={{32,0},{64,32},{96,64},{128,96},{160,128},{192,160},{224,192},{256... | collective-permute-start | bytes 36872 | tf_op jit(solution)/shard_map/ppermute | solution.py:15
  82.0 2.4 %collective-permute-start.17 = (f32[1,24,128]{2,1,0:T(8,128)S(1)}, f32[1,24,128]{2,1,0:T(8,128)S(1)}, u32[]{:S(2)}, u32[]{:S(2)}) collective-permute-start(f32[1,24,128]{2,1,0:T(8,128)S(1)} %get-tuple-element.25), channel_id=1, source_target_pairs={{0,32},{32,64},{64,96},{96,128},{128,160},{160,192},{192,224},{224... | collective-permute-start | bytes 36872 | tf_op jit(solution)/shard_map/ppermute | solution.py:14
  84.4 0.2 fusion.60
  84.6 3.6 %collective-permute-done.17 = f32[1,24,128]{2,1,0:T(8,128)S(1)} collective-permute-done((f32[1,24,128]{2,1,0:T(8,128)S(1)}, f32[1,24,128]{2,1,0:T(8,128)S(1)}, u32[]{:S(2)}, u32[]{:S(2)}) %collective-permute-start.17) | collective-permute-done | bytes 12320 | tf_op jit(solution)/shard_map/ppermute | solution.py:14
  88.2 7.5 %collective-permute-start.18 = (f32[26,1,128]{2,1,0:T(1,128)S(1)}, f32[26,1,128]{2,1,0:T(1,128)S(1)}, u32[]{:S(2)}, u32[]{:S(2)}) collective-permute-start(f32[26,1,128]{2,1,0:T(1,128)S(1)} %get-tuple-element.18), channel_id=1, source_target_pairs={{1,0},{2,1},{3,2},{4,3},{5,4},{6,5},{7,6},{8,7},{9,8},{10,9},{11,1... | collective-permute-start | bytes 39944 | tf_op jit(solution)/shard_map/ppermute | solution.py:15
  95.7 1.9 %collective-permute-start.19 = (f32[26,1,128]{2,1,0:T(1,128)S(1)}, f32[26,1,128]{2,1,0:T(1,128)S(1)}, u32[]{:S(2)}, u32[]{:S(2)}) collective-permute-start(f32[26,1,128]{2,1,0:T(1,128)S(1)} %get-tuple-element.17), channel_id=1, source_target_pairs={{0,1},{1,2},{2,3},{3,4},{4,5},{5,6},{6,7},{7,8},{8,9},{9,10},{10,1... | collective-permute-start | bytes 39944 | tf_op jit(solution)/shard_map/ppermute | solution.py:14
  97.7 0.1 fusion.65
  97.8 6.8 %collective-permute-done.19 = f32[26,1,128]{2,1,0:T(1,128)S(1)} collective-permute-done((f32[26,1,128]{2,1,0:T(1,128)S(1)}, f32[26,1,128]{2,1,0:T(1,128)S(1)}, u32[]{:S(2)}, u32[]{:S(2)}) %collective-permute-start.19) | collective-permute-done | bytes 13344 | tf_op jit(solution)/shard_map/ppermute | solution.py:14
  104.6 4.6 %add_bitcast_fusion = f32[1,24,24,128]{3,2,1,0:T(8,128)S(1)} fusion(f32[24,24,128]{2,1,0:T(8,128)S(1)} %get-tuple-element.5, pred[24,24,128]{2,1,0:T(8,128)(4,1)S(1)} %get-tuple-element.8, pred[24,24,128]{2,1,0:T(8,128)(4,1)S(1)} %get-tuple-element.7, pred[24,24,128]{2,1,0:T(8,128)(4,1)S(1)} %get-tuple-element.6, f32[24,24,128]{2,1,0:T(8,128)S(1)} %fusion.55, ...), kind=kLoop, calls=%fused_computation.96 | loop fusion | flops 4718592 | bytes 2993176 | tf_op jit(solution)/shard_map/stack | solution.py:103
  109.2 0.9 pad_maximum_fusion.2
  110.1 2.9 %fusion.14 = f32[24,24,128]{2,1,0:T(8,128)} fusion(f32[26,26,128]{2,1,0:T(8,128)S(1)} %get-tuple-element.16, f32[26,26,128]{2,1,0:T(8,128)S(1)} %get-tuple-element.15, f32[24,24,128]{2,1,0:T(8,128)S(1)} %copy-done, f32[1,24,128]{2,1,0:T(8,128)S(1)} %collective-permute-done.10, f32[1,24,128]{2,1,0:T(8,128)S(1)} %collective-permute-done, ...), kind=kLoop, calls=%fused_computation.34 | loop fusion | flops 8110080 | bytes 7527936 | tf_op jit(solution)/shard_map/sub | solution.py:99
  (45 shorter events, 0.3 us)
Async XLA Ops:
  0.6 22.7 %copy-start.1 = (bf16[2,24,24,128]{3,2,1,0:T(8,128)(2,1)S(1)}, bf16[2,24,24,128]{3,2,1,0:T(8,128)(2,1)}, u32[]{:S(2)}) copy-start(bf16[2,24,24,128]{3,2,1,0:T(8,128)(2,1)} %param.19) | copy-start | bytes 884740
  0.6 28.7 %copy-start = (f32[24,24,128]{2,1,0:T(8,128)S(1)}, f32[24,24,128]{2,1,0:T(8,128)}, u32[]{:S(2)}) copy-start(f32[24,24,128]{2,1,0:T(8,128)} %param.13) | copy-start | bytes 884740
  0.7 18.3 %copy-start.3 = (f32[3]{0:T(128)S(1)}, f32[3]{0:T(128)}, u32[]{:S(2)}) copy-start(f32[3]{0:T(128)} %param.15) | copy-start | bytes 40
  0.7 18.9 %copy-start.5 = (f32[63]{0:T(128)S(1)}, f32[63]{0:T(128)}, u32[]{:S(2)}) copy-start(f32[63]{0:T(128)} %param.18) | copy-start | bytes 760
  0.7 19.4 %copy-start.6 = (f32[31]{0:T(128)S(1)}, f32[31]{0:T(128)}, u32[]{:S(2)}) copy-start(f32[31]{0:T(128)} %param.17) | copy-start | bytes 376
  0.7 19.4 %copy-start.7 = (f32[31]{0:T(128)S(1)}, f32[31]{0:T(128)}, u32[]{:S(2)}) copy-start(f32[31]{0:T(128)} %param.16) | copy-start | bytes 376
  0.7 19.5 %copy-start.4 = (f32[3]{0:T(128)S(1)}, f32[3]{0:T(128)}, u32[]{:S(2)}) copy-start(f32[3]{0:T(128)} %param.14) | copy-start | bytes 40
  1.6 19.3 %collective-permute-start.1 = (bf16[2,1,24,128]{3,2,1,0:T(8,128)(2,1)S(1)}, bf16[2,1,24,128]{3,2,1,0:T(8,128)(2,1)S(1)}, u32[]{:S(2)}, u32[]{:S(2)}) collective-permute-start(bf16[2,1,24,128]{3,2,1,0:T(8,128)(2,1)S(1)} %get-tuple-element.40), channel_id=1, source_target_pairs={{0,32},{32,64},{64,96},{96,128},{128,160},{160,192},{192,224},{224... | collective-permute-start | bytes 36872 | tf_op jit(solution)/shard_map/ppermute | solution.py:14
  3.5 19.9 %collective-permute-start.2 = (bf16[2,1,24,128]{3,2,1,0:T(8,128)(2,1)S(1)}, bf16[2,1,24,128]{3,2,1,0:T(8,128)(2,1)S(1)}, u32[]{:S(2)}, u32[]{:S(2)}) collective-permute-start(bf16[2,1,24,128]{3,2,1,0:T(8,128)(2,1)S(1)} %get-tuple-element.39), channel_id=1, source_target_pairs={{32,0},{64,32},{96,64},{128,96},{160,128},{192,160},{224,192},{256... | collective-permute-start | bytes 36872 | tf_op jit(solution)/shard_map/ppermute | solution.py:15
  9.1 18.2 %collective-permute-start.10 = (f32[1,24,128]{2,1,0:T(8,128)S(1)}, f32[1,24,128]{2,1,0:T(8,128)S(1)}, u32[]{:S(2)}, u32[]{:S(2)}) collective-permute-start(f32[1,24,128]{2,1,0:T(8,128)S(1)} %get-tuple-element.38), channel_id=1, source_target_pairs={{0,32},{32,64},{64,96},{96,128},{128,160},{160,192},{192,224},{224... | collective-permute-start | bytes 36872 | tf_op jit(solution)/shard_map/ppermute | solution.py:14
  11.0 27.6 %collective-permute-start = (f32[1,24,128]{2,1,0:T(8,128)S(1)}, f32[1,24,128]{2,1,0:T(8,128)S(1)}, u32[]{:S(2)}, u32[]{:S(2)}) collective-permute-start(f32[1,24,128]{2,1,0:T(8,128)S(1)} %get-tuple-element.37), channel_id=1, source_target_pairs={{32,0},{64,32},{96,64},{128,96},{160,128},{192,160},{224,192},{256... | collective-permute-start | bytes 36872 | tf_op jit(solution)/shard_map/ppermute | solution.py:15
  17.0 12.4 %collective-permute-start.6 = (f32[15,24,128]{2,1,0:T(8,128)S(1)}, f32[15,24,128]{2,1,0:T(8,128)S(1)}, u32[]{:S(2)}, u32[]{:S(2)}) collective-permute-start(f32[15,24,128]{2,1,0:T(8,128)S(1)} %get-tuple-element.36), channel_id=1, source_target_pairs={{32,0},{64,32},{96,64},{128,96},{160,128},{192,160},{224,192},{256... | collective-permute-start | bytes 552968 | tf_op jit(solution)/shard_map/ppermute | solution.py:15
  20.9 8.5 %collective-permute-start.5 = (f32[15,24,128]{2,1,0:T(8,128)S(1)}, f32[15,24,128]{2,1,0:T(8,128)S(1)}, u32[]{:S(2)}, u32[]{:S(2)}) collective-permute-start(f32[15,24,128]{2,1,0:T(8,128)S(1)} %get-tuple-element.35), channel_id=1, source_target_pairs={{0,32},{32,64},{64,96},{96,128},{128,160},{160,192},{192,224},{224... | collective-permute-start | bytes 552968 | tf_op jit(solution)/shard_map/ppermute | solution.py:14
  23.5 17.1 %collective-permute-start.4 = (bf16[2,26,1,128]{3,2,1,0:T(2,128)(2,1)S(1)}, bf16[2,26,1,128]{3,2,1,0:T(2,128)(2,1)S(1)}, u32[]{:S(2)}, u32[]{:S(2)}) collective-permute-start(bf16[2,26,1,128]{3,2,1,0:T(2,128)(2,1)S(1)} %get-tuple-element.24), channel_id=1, source_target_pairs={{1,0},{2,1},{3,2},{4,3},{5,4},{6,5},{7,6},{8,7},{9,8},{10,9},{11,1... | collective-permute-start | bytes 39944 | tf_op jit(solution)/shard_map/ppermute | solution.py:15
  27.2 20.5 %collective-permute-start.3 = (bf16[2,26,1,128]{3,2,1,0:T(2,128)(2,1)S(1)}, bf16[2,26,1,128]{3,2,1,0:T(2,128)(2,1)S(1)}, u32[]{:S(2)}, u32[]{:S(2)}) collective-permute-start(bf16[2,26,1,128]{3,2,1,0:T(2,128)(2,1)S(1)} %get-tuple-element.23), channel_id=1, source_target_pairs={{0,1},{1,2},{2,3},{3,4},{4,5},{5,6},{6,7},{7,8},{8,9},{9,10},{10,1... | collective-permute-start | bytes 39944 | tf_op jit(solution)/shard_map/ppermute | solution.py:14
  29.5 18.5 %collective-permute-start.8 = (f32[54,15,128]{2,1,0:T(8,128)S(1)}, f32[54,15,128]{2,1,0:T(8,128)S(1)}, u32[]{:S(2)}, u32[]{:S(2)}) collective-permute-start(f32[54,15,128]{2,1,0:T(8,128)S(1)} %get-tuple-element.10), channel_id=1, source_target_pairs={{1,0},{2,1},{3,2},{4,3},{5,4},{6,5},{7,6},{8,7},{9,8},{10,9},{11,1... | collective-permute-start | bytes 1244168 | tf_op jit(solution)/shard_map/ppermute | solution.py:15
  36.6 16.6 %collective-permute-start.7 = (f32[54,15,128]{2,1,0:T(8,128)S(1)}, f32[54,15,128]{2,1,0:T(8,128)S(1)}, u32[]{:S(2)}, u32[]{:S(2)}) collective-permute-start(f32[54,15,128]{2,1,0:T(8,128)S(1)} %get-tuple-element.9), channel_id=1, source_target_pairs={{0,1},{1,2},{2,3},{3,4},{4,5},{5,6},{6,7},{7,8},{8,9},{9,10},{10,1... | collective-permute-start | bytes 1244168 | tf_op jit(solution)/shard_map/ppermute | solution.py:14
  38.6 35.6 %collective-permute-start.14 = (f32[26,1,128]{2,1,0:T(1,128)S(1)}, f32[26,1,128]{2,1,0:T(1,128)S(1)}, u32[]{:S(2)}, u32[]{:S(2)}) collective-permute-start(f32[26,1,128]{2,1,0:T(1,128)S(1)} %get-tuple-element.20), channel_id=1, source_target_pairs={{0,1},{1,2},{2,3},{3,4},{4,5},{5,6},{6,7},{7,8},{8,9},{9,10},{10,1... | collective-permute-start | bytes 39944 | tf_op jit(solution)/shard_map/ppermute | solution.py:14
  40.5 33.6 %collective-permute-start.12 = (f32[26,1,128]{2,1,0:T(1,128)S(1)}, f32[26,1,128]{2,1,0:T(1,128)S(1)}, u32[]{:S(2)}, u32[]{:S(2)}) collective-permute-start(f32[26,1,128]{2,1,0:T(1,128)S(1)} %get-tuple-element.19), channel_id=1, source_target_pairs={{1,0},{2,1},{3,2},{4,3},{5,4},{6,5},{7,6},{8,7},{9,8},{10,9},{11,1... | collective-permute-start | bytes 39944 | tf_op jit(solution)/shard_map/ppermute | solution.py:15
  55.4 5.1 %collective-permute-start.9 = (f32[1,24,128]{2,1,0:T(8,128)S(1)}, f32[1,24,128]{2,1,0:T(8,128)S(1)}, u32[]{:S(2)}, u32[]{:S(2)}) collective-permute-start(f32[1,24,128]{2,1,0:T(8,128)S(1)} %get-tuple-element.30), channel_id=1, source_target_pairs={{32,0},{64,32},{96,64},{128,96},{160,128},{192,160},{224,192},{256... | collective-permute-start | bytes 36872 | tf_op jit(solution)/shard_map/ppermute | solution.py:15
  58.5 6.2 %collective-permute-start.11 = (f32[1,24,128]{2,1,0:T(8,128)S(1)}, f32[1,24,128]{2,1,0:T(8,128)S(1)}, u32[]{:S(2)}, u32[]{:S(2)}) collective-permute-start(f32[1,24,128]{2,1,0:T(8,128)S(1)} %get-tuple-element.29), channel_id=1, source_target_pairs={{0,32},{32,64},{64,96},{96,128},{128,160},{160,192},{192,224},{224... | collective-permute-start | bytes 36872 | tf_op jit(solution)/shard_map/ppermute | solution.py:14
  60.5 14.8 %copy-start.2 = (s32[24,24,128]{2,1,0:T(8,128)S(1)}, s32[24,24,128]{2,1,0:T(8,128)}, u32[]{:S(2)}) copy-start(s32[24,24,128]{2,1,0:T(8,128)} %param.12) | copy-start | bytes 884740
  64.7 9.4 %collective-permute-start.15 = (f32[26,1,128]{2,1,0:T(1,128)S(1)}, f32[26,1,128]{2,1,0:T(1,128)S(1)}, u32[]{:S(2)}, u32[]{:S(2)}) collective-permute-start(f32[26,1,128]{2,1,0:T(1,128)S(1)} %get-tuple-element.22), channel_id=1, source_target_pairs={{0,1},{1,2},{2,3},{3,4},{4,5},{5,6},{6,7},{7,8},{8,9},{9,10},{10,1... | collective-permute-start | bytes 39944 | tf_op jit(solution)/shard_map/ppermute | solution.py:14
  66.7 8.6 %collective-permute-start.13 = (f32[26,1,128]{2,1,0:T(1,128)S(1)}, f32[26,1,128]{2,1,0:T(1,128)S(1)}, u32[]{:S(2)}, u32[]{:S(2)}) collective-permute-start(f32[26,1,128]{2,1,0:T(1,128)S(1)} %get-tuple-element.21), channel_id=1, source_target_pairs={{1,0},{2,1},{3,2},{4,3},{5,4},{6,5},{7,6},{8,7},{9,8},{10,9},{11,1... | collective-permute-start | bytes 39944 | tf_op jit(solution)/shard_map/ppermute | solution.py:15
  80.0 4.6 %collective-permute-start.16 = (f32[1,24,128]{2,1,0:T(8,128)S(1)}, f32[1,24,128]{2,1,0:T(8,128)S(1)}, u32[]{:S(2)}, u32[]{:S(2)}) collective-permute-start(f32[1,24,128]{2,1,0:T(8,128)S(1)} %get-tuple-element.26), channel_id=1, source_target_pairs={{32,0},{64,32},{96,64},{128,96},{160,128},{192,160},{224,192},{256... | collective-permute-start | bytes 36872 | tf_op jit(solution)/shard_map/ppermute | solution.py:15
  82.0 6.2 %collective-permute-start.17 = (f32[1,24,128]{2,1,0:T(8,128)S(1)}, f32[1,24,128]{2,1,0:T(8,128)S(1)}, u32[]{:S(2)}, u32[]{:S(2)}) collective-permute-start(f32[1,24,128]{2,1,0:T(8,128)S(1)} %get-tuple-element.25), channel_id=1, source_target_pairs={{0,32},{32,64},{64,96},{96,128},{128,160},{160,192},{192,224},{224... | collective-permute-start | bytes 36872 | tf_op jit(solution)/shard_map/ppermute | solution.py:14
  88.2 9.6 %collective-permute-start.18 = (f32[26,1,128]{2,1,0:T(1,128)S(1)}, f32[26,1,128]{2,1,0:T(1,128)S(1)}, u32[]{:S(2)}, u32[]{:S(2)}) collective-permute-start(f32[26,1,128]{2,1,0:T(1,128)S(1)} %get-tuple-element.18), channel_id=1, source_target_pairs={{1,0},{2,1},{3,2},{4,3},{5,4},{6,5},{7,6},{8,7},{9,8},{10,9},{11,1... | collective-permute-start | bytes 39944 | tf_op jit(solution)/shard_map/ppermute | solution.py:15
  95.7 8.9 %collective-permute-start.19 = (f32[26,1,128]{2,1,0:T(1,128)S(1)}, f32[26,1,128]{2,1,0:T(1,128)S(1)}, u32[]{:S(2)}, u32[]{:S(2)}) collective-permute-start(f32[26,1,128]{2,1,0:T(1,128)S(1)} %get-tuple-element.17), channel_id=1, source_target_pairs={{0,1},{1,2},{2,3},{3,4},{4,5},{5,6},{6,7},{7,8},{8,9},{9,10},{10,1... | collective-permute-start | bytes 39944 | tf_op jit(solution)/shard_map/ppermute | solution.py:14
where the time goes:
time: 114 us; the launch traced here: 113 us
  starting transfers between devices  69.7 us (61%)
  waiting for transfers between devices  20.9 us (18%)
  other arithmetic  15.3 us (13%)
  local copies, waits for them, and re-layouts  3.76 us (3%)
  matrix products  2.04 us (2%)
  between operations  1.2 us (1%)
    ppermute x10, starting transfers between devices, padded(): after = lax.ppermute(first, axis, down)  49.4 us
    ppermute x10, starting transfers between devices, padded(): before = lax.ppermute(last, axis, up)  20.3 us
    ppermute x10, waiting for transfers between devices, padded(): before = lax.ppermute(last, axis, up)  19.8 us
    another operation x3, other arithmetic, shards(): return (diff_grad, jnp.stack([adj_free, adj_bound]))  10.1 us
    sub x1, other arithmetic, shards(): diff_grad = diff_grad - slope * (state_other - state) * change  2.92 us
  transfers between devices with their start and end apart: 20, of which 5 were waited for; matrix products, arithmetic and copies ran while one was open for 6% of the time, Pallas kernels for 0%

commit v1 on v0

v1 whole, which is shorter than its diff:
```python
import functools

import jax
import jax.numpy as jnp
from jax import lax
from jax.experimental import pallas as pl
from jax.experimental.pallas import tpu as pltpu
from jax.sharding import PartitionSpec as P

AXES = ("gx", "gy")
RIM = 2
JOFF = 4
SLOT = 32


def blur(read, write, taps, count, span, group):
    for start in range(0, count, group):
        outs = range(start, min(start + group, count))
        acc = {}
        for e in range(outs[0], outs[-1] + span):
            value = read(e)
            for i in outs:
                if 0 <= e - i < span:
                    term = taps[e - i] * value
                    acc[i] = acc[i] + term if i in acc else term
            if e - (span - 1) in acc:
                i = e - (span - 1)
                write(i, acc.pop(i))


def first_kernel(reach, misfit, mask, labels, diffusion, states, kern_z, own, one, two, zrow, work, edge):
    rows_x = states.shape[1]
    depth = misfit.shape[1]
    nx, ny = rows_x, misfit.shape[0] // rows_x
    taps_z = kern_z.shape[1]
    half = (taps_z - 1) // 2
    zrow[...] = jnp.zeros_like(zrow)
    zrow[0:1, 0:taps_z] = kern_z[...]
    spread = jnp.broadcast_to(zrow[0:1, :], (depth, depth))
    rolled = pltpu.roll(spread, depth - half, 1, stride=1, stride_axis=0)
    w = lax.broadcasted_iota(jnp.int32, (depth, depth), 0)
    z = lax.broadcasted_iota(jnp.int32, (depth, depth), 1)
    matrix = jnp.where(jnp.abs(z - w) <= half, rolled, 0.0)
    weighted = (1.0 + 3.0 * mask[...].astype(jnp.float32)) * misfit[...]
    work[...] = lax.dot_general(
        weighted, matrix, (((1,), (1,)), ((), ())),
        precision=lax.Precision.HIGHEST, preferred_element_type=jnp.float32)
    edge[...] = states[...].astype(jnp.float32).reshape(edge.shape)
    octets = nx // 8
    for y in range(ny):
        for o in range(octets):
            own[y, pl.ds(8 * o, 8), :] = work[pl.ds(8 * o * ny + y, 8, stride=ny), :]
    right_first = (lax.axis_index("gx") + lax.axis_index("gy")) % 2 == 0
    width = reach + RIM

    def pack(out, right):
        start = ny - width if right else 0
        for y in range(width):
            out[y] = own[start + y]
        for k in range(RIM):
            y = ny - RIM + k if right else k
            for o in range(octets):
                out[width + k, pl.ds(8 * o, 8), :] = diffusion[pl.ds(8 * o * ny + y, 8, stride=ny), :]
        y = ny - 1 if right else 0
        for o in range(octets):
            here = pl.ds(8 * o * ny + y, 8, stride=ny)
            out[width + RIM, pl.ds(8 * o, 8), :] = labels[here, :].astype(jnp.float32)
            for s in range(states.shape[0]):
                at = pl.ds((s * nx + 8 * o) * ny + y, 8, stride=ny)
                out[width + RIM + 1 + s, pl.ds(8 * o, 8), :] = edge[at, :]

    @pl.when(right_first)
    def _():
        pack(one, True)
        pack(two, False)

    @pl.when(jnp.logical_not(right_first))
    def _():
        pack(one, False)
        pack(two, True)


def second_kernel(own, one, two, labels, diffusion, states, kern_y, blurred, outer, inner, ext, side):
    ny, nx, depth = own.shape
    span = kern_y.shape[0]
    reach = (span - 1) // 2
    width = reach + RIM
    tall = ny + 2 * RIM
    octets = nx // 8
    right_first = (lax.axis_index("gx") + lax.axis_index("gy")) % 2 == 0

    def place(left, right):
        for y in range(width):
            ext[y] = left[y]
            ext[width + ny + y] = right[y]
        for k in range(left.shape[0] - width):
            side[0, k] = left[width + k]
            side[1, k] = right[width + k]

    @pl.when(right_first)
    def _():
        place(two, one)

    @pl.when(jnp.logical_not(right_first))
    def _():
        place(one, two)

    ext[pl.ds(width, ny)] = own[...]
    taps = [kern_y[t] for t in range(span)]
    for o in range(octets):
        def read(e):
            return ext[e, pl.ds(8 * o, 8), :]

        def write(j, value):
            blurred[pl.ds(8 * o * SLOT + JOFF - RIM + j, 8, stride=SLOT), :] = value

        blur(read, write, taps, tall, span, 14)

    def pack(out, upper):
        at = 0
        first = nx - width if upper else 0
        for x in range(first, first + width):
            out[pl.ds(at, tall), :] = blurred[pl.ds(x * SLOT + JOFF - RIM, tall), :]
            at += tall
        for k in range(RIM):
            x = nx - RIM + k if upper else k
            for r in range(RIM):
                out[pl.ds(at + r, 1), :] = side[0, r, pl.ds(x, 1), :]
                out[pl.ds(at + RIM + ny + r, 1), :] = side[1, r, pl.ds(x, 1), :]
            out[pl.ds(at + RIM, ny), :] = diffusion[x]
            at += tall
        x = nx - 1 if upper else 0
        out[pl.ds(at, ny), :] = labels[x].astype(jnp.float32)
        at += ny
        for s in range(states.shape[0]):
            out[pl.ds(at, ny), :] = states[s, x].astype(jnp.float32)
            at += ny

    even = lax.axis_index("gx") % 2 == 0

    @pl.when(even)
    def _():
        pack(inner, True)
        pack(outer, False)

    @pl.when(jnp.logical_not(even))
    def _():
        pack(inner, False)
        pack(outer, True)


def third_kernel(blurred, outer, inner, one, two, labels, diffusion, states, kern_x, bind_t, release_t,
                 grad, adjoint, ext, image, adj, coef, state, kind):
    nx, ny, depth = labels.shape
    steps = states.shape[0]
    span = kern_x.shape[0]
    reach = (span - 1) // 2
    width = reach + RIM
    tall = ny + 2 * RIM
    octets = nx // 8
    high = image.shape[1]
    right_first = (lax.axis_index("gx") + lax.axis_index("gy")) % 2 == 0
    even = lax.axis_index("gx") % 2 == 0
    lo, n_in = JOFF - RIM, slice(JOFF, JOFF + ny)

    def place(slab, upper):
        at = 0
        base = width + nx if upper else 0
        for k in range(width):
            ext[base + k, lo:lo + tall, :] = slab[pl.ds(at, tall), :]
            at += tall
        order = range(nx + RIM, nx + 2 * RIM) if upper else range(RIM)
        for i in order:
            coef[i, lo:lo + tall, :] = slab[pl.ds(at, tall), :]
            at += tall
        i = nx + 1 if upper else 0
        kind[i, n_in, :] = slab[pl.ds(at, ny), :]
        at += ny
        for s in range(steps):
            state[s, i, n_in, :] = slab[pl.ds(at, ny), :]
            at += ny

    @pl.when(even)
    def _():
        place(outer, False)
        place(inner.at[1], True)

    @pl.when(jnp.logical_not(even))
    def _():
        place(inner.at[0], False)
        place(outer, True)

    for x in range(nx):
        ext[width + x, 0:SLOT, :] = blurred[pl.ds(x * SLOT, SLOT), :]
        coef[RIM + x, n_in, :] = diffusion[x]
        kind[1 + x, n_in, :] = labels[x].astype(jnp.float32)
        for s in range(steps):
            state[s, 1 + x, n_in, :] = states[s, x].astype(jnp.float32)

    def rims(left, right):
        for x in range(nx):
            row = pl.ds(x, 1)
            for k in range(RIM):
                coef[RIM + x, JOFF - RIM + k:JOFF - RIM + k + 1, :] = left[width + k, row, :]
                coef[RIM + x, JOFF + ny + k:JOFF + ny + k + 1, :] = right[width + k, row, :]
            kind[1 + x, JOFF - 1:JOFF, :] = left[width + RIM, row, :]
            kind[1 + x, JOFF + ny:JOFF + ny + 1, :] = right[width + RIM, row, :]
            for s in range(steps):
                state[s, 1 + x, JOFF - 1:JOFF, :] = left[width + RIM + 1 + s, row, :]
                state[s, 1 + x, JOFF + ny:JOFF + ny + 1, :] = right[width + RIM + 1 + s, row, :]

    @pl.when(right_first)
    def _():
        rims(two, one)

    @pl.when(jnp.logical_not(right_first))
    def _():
        rims(one, two)

    taps = [kern_x[t] for t in range(span)]

    @pl.loop(0, SLOT // 8)
    def _(v):
        rows = pl.ds(pl.multiple_of(8 * v, 8), 8)

        def write(i, value):
            image[i, rows, :] = value

        blur(lambda e: ext[e, rows, :], write, taps, nx + 2 * RIM, span, 14)

    def rate(code, table):
        return jnp.where(code == 0, table[0], jnp.where(code == 1, table[1], table[2]))

    def inside(rows):
        return lax.broadcasted_iota(jnp.int32, (rows, depth), 1) < depth - 1

    def ratio(here, there):
        inverse = 1.0 / jnp.maximum(here + there, 1e-30)
        return there * inverse, here * inverse

    @pl.loop(0, nx + 2)
    def _(i):
        h = slice(JOFF - 2, JOFF - 2 + SLOT)
        a, d = image[i + 1, h, :], coef[i + 1, h, :]

        def flux(a_there, d_there):
            q, _ = ratio(d, d_there)
            return 2.0 * d * q * (a_there - a)

        last = inside(SLOT)
        up = JOFF - 1
        total = flux(image[i + 2, h, :], coef[i + 2, h, :]) + flux(image[i, h, :], coef[i, h, :])
        total += flux(image[i + 1, up:up + SLOT, :], coef[i + 1, up:up + SLOT, :])
        total += flux(image[i + 1, up - 2:up - 2 + SLOT, :], coef[i + 1, up - 2:up - 2 + SLOT, :])
        fz = jnp.where(last, flux(pltpu.roll(a, depth - 1, 1), pltpu.roll(d, depth - 1, 1)), 0.0)
        total += fz - pltpu.roll(fz, 1, 1)
        bind = rate(kind[i, h, :], bind_t)
        adj[i, h, :] = a + total - 0.5 * bind * a

    @pl.loop(0, nx)
    def _(x):
        i = x + 1
        h = n_in
        d, a1, a0 = coef[i + 1, h, :], image[i + 1, h, :], adj[i, h, :]
        s1, s0 = state[steps - 1, i, h, :], state[0, i, h, :]

        def face(di, shift):
            g = slice(JOFF + shift, JOFF + shift + ny)
            q, _ = ratio(d, coef[i + 1 + di, g, :])
            change1 = image[i + 1 + di, g, :] - a1
            change0 = adj[i + di, g, :] - a0
            both = (state[steps - 1, i + di, g, :] - s1) * change1 + (state[0, i + di, g, :] - s0) * change0
            return d * q * change0, q * q * both

        total, slopes = face(1, 0)
        for di, shift in ((-1, 0), (0, 1), (0, -1)):
            f, p = face(di, shift)
            total, slopes = total + f, slopes + p
        last = inside(ny)
        nxt = functools.partial(pltpu.roll, shift=depth - 1, axis=1)
        q, p = ratio(d, nxt(d))
        change1, change0 = nxt(a1) - a1, nxt(a0) - a0
        both = jnp.where(last, (nxt(s1) - s1) * change1 + (nxt(s0) - s0) * change0, 0.0)
        fz = jnp.where(last, d * q * change0, 0.0)
        total += fz - pltpu.roll(fz, 1, 1)
        slopes += q * q * both + pltpu.roll(p * p * both, 1, 1)
        code = labels[x]
        bind, release = rate(code, bind_t), rate(code, release_t)
        b1 = 0.5 * a1 + release * (a1 - 0.5 * a1)
        grad[x] = -2.0 * slopes
        adjoint[0, x] = a0 + 2.0 * total + bind * (b1 - a0)
        adjoint[1, x] = b1 + release * (a0 - b1)


def swap_along_gy(shape, parity):
    nx, ny = shape
    pairs = []
    for i in range(nx):
        for j in range((parity + i) % 2, ny - 1, 2):
            a, b = i * ny + j, i * ny + j + 1
            pairs += [(a, b), (b, a)]
    return pairs


def shards(misfit, bleach_mask, labels, diffusion, bind_table, release_table, kern_x, kern_y, kern_z, free_states):
    nx, ny, depth = misfit.shape
    steps = free_states.shape[0]
    reach = (kern_x.shape[0] - 1) // 2
    width = reach + RIM
    tall = ny + 2 * RIM
    shape = (lax.axis_size("gx"), lax.axis_size("gy"))
    f32 = jnp.float32
    vmem = pl.BlockSpec(memory_space=pltpu.VMEM)
    smem = pl.BlockSpec(memory_space=pltpu.SMEM)
    params = pltpu.CompilerParams(vmem_limit_bytes=40 * 1024 * 1024)
    flat = (nx * ny, depth)

    slots = width + RIM + 1 + steps
    slab = jax.ShapeDtypeStruct((slots, nx, depth), f32)
    own, one, two = pl.pallas_call(
        functools.partial(first_kernel, reach),
        out_shape=[jax.ShapeDtypeStruct((ny, nx, depth), f32), slab, slab],
        in_specs=[vmem] * 6,
        out_specs=[vmem] * 3,
        scratch_shapes=[pltpu.VMEM((8, depth), f32), pltpu.VMEM(flat, f32), pltpu.VMEM((steps * nx * ny, depth), f32)],
        compiler_params=params,
        name="weigh_blur_z",
    )(misfit.reshape(flat), bleach_mask.reshape(flat), labels.reshape(flat), diffusion.reshape(flat), free_states,
      kern_z.reshape(1, -1))
    one = lax.ppermute(one, AXES, swap_along_gy(shape, 0))
    two = lax.ppermute(two, AXES, swap_along_gy(shape, 1))

    rows = (width + RIM) * tall + (1 + steps) * ny
    slab = jax.ShapeDtypeStruct((rows, depth), f32)
    blurred, outer, inner = pl.pallas_call(
        second_kernel,
        out_shape=[jax.ShapeDtypeStruct((nx * SLOT, depth), f32), slab, slab],
        in_specs=[vmem] * 6 + [smem],
        out_specs=[vmem] * 3,
        scratch_shapes=[pltpu.VMEM((ny + 2 * width, nx, depth), f32), pltpu.VMEM((2, slots - width, nx, depth), f32)],
        compiler_params=params,
        name="blur_y",
    )(own, one, two, labels, diffusion, free_states, kern_y)

    line = shape[1]
    across = []
    for i in range(1, shape[0] - 1, 2):
        for j in range(line):
            a, b = i * line + j, (i + 1) * line + j
            across += [(a, b), (b, a)]
    within = [[i * line + j, (i + 1) * line + j] for i in range(0, shape[0], 2) for j in range(line)]
    outer = lax.ppermute(outer, AXES, across)
    inner = lax.all_gather(inner, AXES, axis_index_groups=within)

    high = SLOT + 8
    grad, adjoint = pl.pallas_call(
        third_kernel,
        out_shape=[jax.ShapeDtypeStruct((nx, ny, depth), f32), jax.ShapeDtypeStruct((2, nx, ny, depth), f32)],
        in_specs=[vmem] * 8 + [smem] * 3,
        out_specs=[vmem] * 2,
        scratch_shapes=[
            pltpu.VMEM((nx + 2 * width, SLOT, depth), f32),
            pltpu.VMEM((nx + 2 * RIM, high, depth), f32),
            pltpu.VMEM((nx + 2, high, depth), f32),
            pltpu.VMEM((nx + 2 * RIM, high, depth), f32),
            pltpu.VMEM((steps, nx + 2, high, depth), f32),
            pltpu.VMEM((nx + 2, high, depth), f32),
        ],
        compiler_params=params,
        name="blur_x_steps",
    )(blurred, outer, inner, one, two, labels, diffusion, free_states, kern_x, bind_table, release_table)
    return grad, adjoint


def solution(mesh):
    tile = P("gx", "gy", None)
    in_specs = (tile, tile, tile, tile, P(), P(), P(), P(), P(), P(None, "gx", "gy", None))
    out_specs = (tile, P(None, "gx", "gy", None))
    return jax.shard_map(shards, mesh=mesh, in_specs=in_specs, out_specs=out_specs, check_vma=False)
```

time: 114 us -> 43.9 us (0.39)
  the two profiles are of different devices: /device:TPU:288 before, /device:TPU:281 now
where the time goes in v1:
time: 43.9 us; the launch traced here: 43.6 us
  starting transfers between devices  15.1 us (34%)
  Pallas kernels  12.8 us (29%)
  waiting for transfers between devices  7.29 us (17%)
  local copies, waits for them, and re-layouts  5.48 us (12%)
  blocking collectives  2.25 us (5%)
  between operations  0.71 us (2%)
    pallas_call x1, Pallas kernels, shards(): pl.pallas_call(third_kernel, out_shape=[jax.ShapeDtypeStruct((nx, ny, dep...  10.8 us
    ppermute x1, starting transfers between devices, shards(): outer = lax.ppermute(outer, AXES, across)  8.83 us
    unnamed x26, local copies, waits for them, and re-layouts  5.48 us
    ppermute x1, waiting for transfers between devices, shards(): one = lax.ppermute(one, AXES, swap_along_gy(shape, 0))  4.26 us
    ppermute x1, starting transfers between devices, shards(): one = lax.ppermute(one, AXES, swap_along_gy(shape, 0))  3.48 us
    ppermute x1, starting transfers between devices, shards(): two = lax.ppermute(two, AXES, swap_along_gy(shape, 1))  2.76 us
    ppermute x1, waiting for transfers between devices, shards(): outer = lax.ppermute(outer, AXES, across)  2.31 us
    all_gather x1, blocking collectives, shards(): inner = lax.all_gather(inner, AXES, axis_index_groups=within)  2.25 us
  transfers between devices with their start and end apart: 3, of which 3 were waited for; matrix products, arithmetic and copies ran while one was open for 0% of the time, Pallas kernels for 0%

profile of v1, /device:TPU:281, one launch (start us, length us, event | category | flops | bytes accessed | tf_op | source)
XLA Modules:
  0.0 43.6 jit_solution(12106116284321360696)
XLA Ops:
  0.6 0.0 copy-start.9
  0.6 0.6 %copy-done.9 = f32[63]{0:T(128)S(1)} copy-done((f32[63]{0:T(128)S(1)}, f32[63]{0:T(128)}, u32[]{:S(2)}) %copy-start.9) | copy-done | bytes 276
  1.3 0.0 copy-start
  1.3 1.0 %copy-done = s32[24,24,128]{2,1,0:T(8,128)S(1)} copy-done((s32[24,24,128]{2,1,0:T(8,128)S(1)}, s32[24,24,128]{2,1,0:T(8,128)}, u32[]{:S(2)}) %copy-start) | copy-done | bytes 294936
  2.2 0.0 copy-start.2
  2.3 1.0 %copy-done.2 = f32[24,24,128]{2,1,0:T(8,128)S(1)} copy-done((f32[24,24,128]{2,1,0:T(8,128)S(1)}, f32[24,24,128]{2,1,0:T(8,128)}, u32[]{:S(2)}) %copy-start.2) | copy-done | bytes 294936
  3.2 0.0 copy-start.4
  3.2 1.0 %copy-done.4 = bf16[2,24,24,128]{3,2,1,0:T(8,128)(2,1)S(1)} copy-done((bf16[2,24,24,128]{3,2,1,0:T(8,128)(2,1)S(1)}, bf16[2,24,24,128]{3,2,1,0:T(8,128)(2,1)}, u32[]{:S(2)}) %copy-start.4) | copy-done | bytes 294936
  4.2 0.0 copy-start.6
  4.2 1.0 %copy-done.6 = f32[24,24,128]{2,1,0:T(8,128)S(1)} copy-done((f32[24,24,128]{2,1,0:T(8,128)S(1)}, f32[24,24,128]{2,1,0:T(8,128)}, u32[]{:S(2)}) %copy-start.6) | copy-done | bytes 294936
  5.1 0.0 copy-start.7
  5.1 1.0 %copy-done.7 = s32[24,24,128]{2,1,0:T(8,128)S(1)} copy-done((s32[24,24,128]{2,1,0:T(8,128)S(1)}, s32[24,24,128]{2,1,0:T(8,128)}, u32[]{:S(2)}) %copy-start.7) | copy-done | bytes 294936
  6.1 0.0 copy-start.1
  6.1 0.0 copy-start.3
  6.1 0.0 copy-start.5
  6.1 0.6 %weigh_blur_z.1 = (f32[24,24,128]{2,1,0:T(8,128)S(1)}, f32[22,24,128]{2,1,0:T(8,128)S(1)}, f32[22,24,128]{2,1,0:T(8,128)S(1)}) custom-call(f32[576,128]{1,0:T(8,128)S(1)} %bitcast.9, s32[576,128]{1,0:T(8,128)S(1)} %bitcast.10, s32[576,128]{1,0:T(8,128)S(1)} %bitcast.6, f32[576,128]{1,0:T(8,128)S(1)} %bitcast.7, bf16[2,24,24,128]{3,2,1,0:T(8,128)(2,1)S(1)} %copy-done.4, ...), custom_call_target="tpu_custom_call" | custom-call | tf_op jit(solution)/shard_map/weigh_blur_z/pallas_call | solution.py:320
  6.7 3.5 %collective-permute-start = (f32[22,24,128]{2,1,0:T(8,128)S(1)}, f32[22,24,128]{2,1,0:T(8,128)S(1)}, u32[]{:S(2)}, u32[]{:S(2)}) collective-permute-start(f32[22,24,128]{2,1,0:T(8,128)S(1)} %get-tuple-element.9), channel_id=1, source_target_pairs={{0,1},{1,0},{2,3},{3,2},{4,5},{5,4},{6,7},{7,6},{8,9},{9,8},{10,11... | collective-permute-start | bytes 811016 | tf_op jit(solution)/shard_map/ppermute | solution.py:330
  10.2 0.0 copy-start.8
  10.2 2.8 %collective-permute-start.1 = (f32[22,24,128]{2,1,0:T(8,128)S(1)}, f32[22,24,128]{2,1,0:T(8,128)S(1)}, u32[]{:S(2)}, u32[]{:S(2)}) collective-permute-start(f32[22,24,128]{2,1,0:T(8,128)S(1)} %get-tuple-element.10), channel_id=1, source_target_pairs={{1,2},{2,1},{3,4},{4,3},{5,6},{6,5},{7,8},{8,7},{9,10},{10,9},{11,... | collective-permute-start | bytes 811016 | tf_op jit(solution)/shard_map/ppermute | solution.py:331
  12.9 4.3 %collective-permute-done.one = f32[22,24,128]{2,1,0:T(8,128)S(1)} collective-permute-done((f32[22,24,128]{2,1,0:T(8,128)S(1)}, f32[22,24,128]{2,1,0:T(8,128)S(1)}, u32[]{:S(2)}, u32[]{:S(2)}) %collective-permute-start) | collective-permute-done | bytes 270368 | tf_op jit(solution)/shard_map/ppermute | solution.py:330
  17.2 0.7 %collective-permute-done.1.two = f32[22,24,128]{2,1,0:T(8,128)S(1)} collective-permute-done((f32[22,24,128]{2,1,0:T(8,128)S(1)}, f32[22,24,128]{2,1,0:T(8,128)S(1)}, u32[]{:S(2)}, u32[]{:S(2)}) %collective-permute-start.1) | collective-permute-done | bytes 270368 | tf_op jit(solution)/shard_map/ppermute | solution.py:331
  17.9 0.0 copy-done.1
  17.9 0.0 copy-done.3
  17.9 0.0 copy-done.5
  17.9 0.0 copy-done.8
  17.9 1.4 %blur_y.1 = (f32[768,128]{1,0:T(8,128)S(1)}, f32[604,128]{1,0:T(8,128)S(1)}, f32[604,128]{1,0:T(8,128)S(1)}) custom-call(f32[24,24,128]{2,1,0:T(8,128)S(1)} %get-tuple-element.8.own, f32[22,24,128]{2,1,0:T(8,128)S(1)} %collective-permute-done.one, f32[22,24,128]{2,1,0:T(8,128)S(1)} %collective-permute-done.1.two, s32[24,24,128]{2,1,0:T(8,128)S(1)} %copy-done.1, ...), custom_call_target="tpu_custom_call" | custom-call | tf_op jit(solution)/shard_map/blur_y/pallas_call | solution.py:335
  19.3 8.8 %collective-permute-start.2 = (f32[604,128]{1,0:T(8,128)S(1)}, f32[604,128]{1,0:T(8,128)S(1)}, u32[]{:S(2)}, u32[]{:S(2)}) collective-permute-start(f32[604,128]{1,0:T(8,128)S(1)} %get-tuple-element.12), channel_id=1, source_target_pairs={{32,64},{64,32},{33,65},{65,33},{34,66},{66,34},{35,67},{67,35},{3... | collective-permute-start | bytes 927752 | tf_op jit(solution)/shard_map/ppermute | solution.py:352
  28.2 2.3 %all-gather.1.inner = f32[2,604,128]{2,1,0:T(8,128)S(1)} all-gather(f32[1,604,128]{2,1,0:T(8,128)S(1)} %bitcast.8), channel_id=2, replica_groups={{0,32},{1,33},{2,34},{3,35},{4,36},{5,37},{6,38},{7,39},{8,40},{9,41},{..., dimensions={0}, use_global_device_ids=true | all-gather | bytes 927744 | tf_op jit(solution)/shard_map/all_gather | solution.py:353
  30.4 0.0 copy-start.10
  30.4 0.0 copy-start.11
  30.4 0.0 copy-start.12
  30.4 2.3 %collective-permute-done.2.outer = f32[604,128]{1,0:T(8,128)S(1)} collective-permute-done((f32[604,128]{1,0:T(8,128)S(1)}, f32[604,128]{1,0:T(8,128)S(1)}, u32[]{:S(2)}, u32[]{:S(2)}) %collective-permute-start.2) | collective-permute-done | bytes 309280 | tf_op jit(solution)/shard_map/ppermute | solution.py:352
  32.8 0.0 copy-done.10
  32.8 0.0 copy-done.11
  32.8 0.0 copy-done.12
  32.8 10.8 %blur_x_steps.1 = (f32[24,24,128]{2,1,0:T(8,128)}, f32[2,24,24,128]{3,2,1,0:T(8,128)}) custom-call(f32[768,128]{1,0:T(8,128)S(1)} %get-tuple-element.11.blurred, f32[604,128]{1,0:T(8,128)S(1)} %collective-permute-done.2.outer, f32[2,604,128]{2,1,0:T(8,128)S(1)} %all-gather.1.inner, f32[22,24,128]{2,1,0:T(8,128)S(1)} %collective-permute-done.one, ...), custom_call_target="tpu_custom_call" | custom-call | tf_op jit(solution)/shard_map/blur_x_steps/pallas_call | solution.py:356
Async XLA Ops:
  0.6 0.7 %copy-start.9 = (f32[63]{0:T(128)S(1)}, f32[63]{0:T(128)}, u32[]{:S(2)}) copy-start(f32[63]{0:T(128)} %param.18) | copy-start | bytes 760
  1.3 1.0 %copy-start = (s32[24,24,128]{2,1,0:T(8,128)S(1)}, s32[24,24,128]{2,1,0:T(8,128)}, u32[]{:S(2)}) copy-start(s32[24,24,128]{2,1,0:T(8,128)} %labels.3) | copy-start | bytes 884740
  2.2 1.0 %copy-start.2 = (f32[24,24,128]{2,1,0:T(8,128)S(1)}, f32[24,24,128]{2,1,0:T(8,128)}, u32[]{:S(2)}) copy-start(f32[24,24,128]{2,1,0:T(8,128)} %diffusion.3) | copy-start | bytes 884740
  3.2 1.0 %copy-start.4 = (bf16[2,24,24,128]{3,2,1,0:T(8,128)(2,1)S(1)}, bf16[2,24,24,128]{3,2,1,0:T(8,128)(2,1)}, u32[]{:S(2)}) copy-start(bf16[2,24,24,128]{3,2,1,0:T(8,128)(2,1)} %states.5) | copy-start | bytes 884740
  4.2 1.0 %copy-start.6 = (f32[24,24,128]{2,1,0:T(8,128)S(1)}, f32[24,24,128]{2,1,0:T(8,128)}, u32[]{:S(2)}) copy-start(f32[24,24,128]{2,1,0:T(8,128)} %param.10) | copy-start | bytes 884740
  5.1 1.0 %copy-start.7 = (s32[24,24,128]{2,1,0:T(8,128)S(1)}, s32[24,24,128]{2,1,0:T(8,128)}, u32[]{:S(2)}) copy-start(s32[24,24,128]{2,1,0:T(8,128)} %param.11) | copy-start | bytes 884740
  6.1 11.8 %copy-start.1 = (s32[24,24,128]{2,1,0:T(8,128)S(1)}, s32[24,24,128]{2,1,0:T(8,128)}, u32[]{:S(2)}) copy-start(s32[24,24,128]{2,1,0:T(8,128)} %labels.3) | copy-start | bytes 884740
  6.1 11.8 %copy-start.3 = (f32[24,24,128]{2,1,0:T(8,128)S(1)}, f32[24,24,128]{2,1,0:T(8,128)}, u32[]{:S(2)}) copy-start(f32[24,24,128]{2,1,0:T(8,128)} %diffusion.3) | copy-start | bytes 884740
  6.1 11.8 %copy-start.5 = (bf16[2,24,24,128]{3,2,1,0:T(8,128)(2,1)S(1)}, bf16[2,24,24,128]{3,2,1,0:T(8,128)(2,1)}, u32[]{:S(2)}) copy-start(bf16[2,24,24,128]{3,2,1,0:T(8,128)(2,1)} %states.5) | copy-start | bytes 884740
  6.7 10.5 %collective-permute-start = (f32[22,24,128]{2,1,0:T(8,128)S(1)}, f32[22,24,128]{2,1,0:T(8,128)S(1)}, u32[]{:S(2)}, u32[]{:S(2)}) collective-permute-start(f32[22,24,128]{2,1,0:T(8,128)S(1)} %get-tuple-element.9), channel_id=1, source_target_pairs={{0,1},{1,0},{2,3},{3,2},{4,5},{5,4},{6,7},{7,6},{8,9},{9,8},{10,11... | collective-permute-start | bytes 811016 | tf_op jit(solution)/shard_map/ppermute | solution.py:330
  10.2 7.8 %copy-start.8 = (f32[31]{0:T(128)S(1)}, f32[31]{0:T(128)}, u32[]{:S(2)}) copy-start(f32[31]{0:T(128)} %kern_y.1) | copy-start | bytes 376
  10.2 7.7 %collective-permute-start.1 = (f32[22,24,128]{2,1,0:T(8,128)S(1)}, f32[22,24,128]{2,1,0:T(8,128)S(1)}, u32[]{:S(2)}, u32[]{:S(2)}) collective-permute-start(f32[22,24,128]{2,1,0:T(8,128)S(1)} %get-tuple-element.10), channel_id=1, source_target_pairs={{1,2},{2,1},{3,4},{4,3},{5,6},{6,5},{7,8},{8,7},{9,10},{10,9},{11,... | collective-permute-start | bytes 811016 | tf_op jit(solution)/shard_map/ppermute | solution.py:331
  19.3 13.4 %collective-permute-start.2 = (f32[604,128]{1,0:T(8,128)S(1)}, f32[604,128]{1,0:T(8,128)S(1)}, u32[]{:S(2)}, u32[]{:S(2)}) collective-permute-start(f32[604,128]{1,0:T(8,128)S(1)} %get-tuple-element.12), channel_id=1, source_target_pairs={{32,64},{64,32},{33,65},{65,33},{34,66},{66,34},{35,67},{67,35},{3... | collective-permute-start | bytes 927752 | tf_op jit(solution)/shard_map/ppermute | solution.py:352
  30.4 2.3 %copy-start.10 = (f32[31]{0:T(128)S(1)}, f32[31]{0:T(128)}, u32[]{:S(2)}) copy-start(f32[31]{0:T(128)} %kern_x.1) | copy-start | bytes 376
  30.4 2.3 %copy-start.11 = (f32[3]{0:T(128)S(1)}, f32[3]{0:T(128)}, u32[]{:S(2)}) copy-start(f32[3]{0:T(128)} %bind_t.1) | copy-start | bytes 40
  30.4 2.3 %copy-start.12 = (f32[3]{0:T(128)S(1)}, f32[3]{0:T(128)}, u32[]{:S(2)}) copy-start(f32[3]{0:T(128)} %release_t.1) | copy-start | bytes 40

commit v2 on v1

v2 whole, which is shorter than its diff:
```python
import functools

import jax
import jax.numpy as jnp
from jax import lax
from jax.experimental import pallas as pl
from jax.experimental.pallas import tpu as pltpu
from jax.sharding import PartitionSpec as P

AXES = ("gx", "gy")
RIM = 2
JOFF = 4
SLOT = 32
HIGH = 40
F32 = jnp.float32


def blur(read, write, taps, outs, sources, group=14, base=None):
    span = len(taps)
    for start in range(0, len(outs), group):
        mine = outs[start:start + group]
        acc = {i: base(i) for i in mine} if base else {}
        for e in sources:
            users = [i for i in mine if 0 <= e - i < span]
            if users:
                value = read(e)
            for i in users:
                term = taps[e - i] * value
                acc[i] = acc[i] + term if i in acc else term
        for i in mine:
            write(i, acc[i])


def right_comes_first():
    return (lax.axis_index("gx") + lax.axis_index("gy")) % 2 == 0


def is_even():
    return lax.axis_index("gx") % 2 == 0


def both_ways(flag, act):
    pl.when(flag)(functools.partial(act, True))
    pl.when(jnp.logical_not(flag))(functools.partial(act, False))


def first_kernel(reach, misfit_h, mask_h, labels_h, diffusion_h, states_h, kern_h, own, one, two,
                 misfit, mask, labels, diffusion, states, kern, work, edge, sems):
    steps, nx, ny, depth = states.shape
    copies = [pltpu.make_async_copy(a, b, sems.at[n]) for n, (a, b) in enumerate(
        ((kern_h, kern), (misfit_h, misfit), (mask_h, mask), (diffusion_h, diffusion), (labels_h, labels), (states_h, states)))]
    for c in copies:
        c.start()
    taps_z = kern.shape[0]
    half = (taps_z - 1) // 2
    copies[0].wait()
    lane = lax.broadcasted_iota(jnp.int32, (8, depth), 1)
    parts = [jnp.zeros((8, depth), F32) for _ in range(4)]
    for t in range(taps_z):
        parts[t % 4] = jnp.where(lane == t, kern[t], parts[t % 4])
    row = (parts[0] + parts[1]) + (parts[2] + parts[3])
    rolled = pltpu.roll(jnp.broadcast_to(row[0:1], (depth, depth)), depth - half, 1, stride=1, stride_axis=0)
    w = lax.broadcasted_iota(jnp.int32, (depth, depth), 0)
    z = lax.broadcasted_iota(jnp.int32, (depth, depth), 1)
    matrix = jnp.where(jnp.abs(z - w) <= half, rolled, 0.0)
    copies[1].wait()
    copies[2].wait()
    weighted = (1.0 + 3.0 * mask[...].astype(F32)) * misfit[...]
    work[...] = lax.dot_general(
        weighted, matrix, (((1,), (1,)), ((), ())),
        precision=lax.Precision.HIGHEST, preferred_element_type=F32)
    for c in copies[3:]:
        c.wait()
    edge[...] = states[...].astype(F32).reshape(edge.shape)
    octets = nx // 8
    for y in range(ny):
        for o in range(octets):
            own[y, pl.ds(8 * o, 8), :] = work[pl.ds(8 * o * ny + y, 8, stride=ny), :]
    width = reach + RIM

    def pack(out, right):
        start = ny - width if right else 0
        for y in range(width):
            out[y] = own[start + y]
        for k in range(RIM):
            y = ny - RIM + k if right else k
            for o in range(octets):
                out[width + k, pl.ds(8 * o, 8), :] = diffusion[pl.ds(8 * o * ny + y, 8, stride=ny), :]
        y = ny - 1 if right else 0
        for o in range(octets):
            here = pl.ds(8 * o * ny + y, 8, stride=ny)
            out[width + RIM, pl.ds(8 * o, 8), :] = labels[here, :].astype(F32)
            for s in range(steps):
                at = pl.ds((s * nx + 8 * o) * ny + y, 8, stride=ny)
                out[width + RIM + 1 + s, pl.ds(8 * o, 8), :] = edge[at, :]

    def act(right):
        pack(one, right)
        pack(two, not right)

    both_ways(right_comes_first(), act)


def own_y_kernel(own, kern_y, part):
    ny, nx, _ = own.shape
    taps = [kern_y[t] for t in range(kern_y.shape[0])]
    width = (len(taps) - 1) // 2 + RIM

    @pl.loop(0, nx // 8)
    def _(o):
        at = pl.ds(pl.multiple_of(8 * o, 8), 8)

        def write(j, value):
            part[j, at, :] = value

        blur(lambda e: own[e - width, at, :], write, taps, range(ny + 2 * RIM), range(width, width + ny))


def rest_y_kernel(part, one, two, labels, diffusion, states, kern_y, blurred, outer, inner, left, right):
    tall, nx, depth = part.shape
    ny = tall - 2 * RIM
    taps = [kern_y[t] for t in range(kern_y.shape[0])]
    width = (len(taps) - 1) // 2 + RIM

    def place(first):
        left[...] = (two if first else one)[...]
        right[...] = (one if first else two)[...]

    both_ways(right_comes_first(), place)

    for o in range(nx // 8):
        at = pl.ds(8 * o, 8)

        def read(e):
            return left[e, at, :] if e < width else right[e - width - ny, at, :]

        def write(j, value):
            blurred[pl.ds(8 * o * SLOT + JOFF - RIM + j, 8, stride=SLOT), :] = value

        blur(read, write, taps, range(tall), [*range(width), *range(width + ny, 2 * width + ny)],
             base=lambda j: part[j, at, :])

    def pack(out, upper):
        at = 0
        order = range(nx - 1, -1, -1) if upper else range(nx)
        for x in order[:width]:
            out[pl.ds(at, tall), :] = blurred[pl.ds(x * SLOT + JOFF - RIM, tall), :]
            at += tall
        for x in order[:RIM]:
            for r in range(RIM):
                out[pl.ds(at + r, 1), :] = left[width + r, pl.ds(x, 1), :]
                out[pl.ds(at + RIM + ny + r, 1), :] = right[width + r, pl.ds(x, 1), :]
            out[pl.ds(at + RIM, ny), :] = diffusion[x]
            at += tall
        x = order[0]
        out[pl.ds(at, ny), :] = labels[x].astype(F32)
        at += ny
        for s in range(states.shape[0]):
            out[pl.ds(at, ny), :] = states[s, x].astype(F32)
            at += ny

    def act(even):
        pack(inner, even)
        pack(outer, not even)

    both_ways(is_even(), act)


def rate(code, table):
    return jnp.where(code == 0, table[0], jnp.where(code == 1, table[1], table[2]))


def shares(here, there):
    inverse = 1.0 / jnp.maximum(here + there, 1e-30)
    return there * inverse, here * inverse


def inside(rows, depth):
    return lax.broadcasted_iota(jnp.int32, (rows, depth), 1) < depth - 1


def early_x_kernel(blurred, inner, one, two, labels, diffusion, states, kern_x, bind_t,
                   image, coef, state, keep, cx, cy, cz, xl, xu, yl, yu, zl, zu, ext, kind):
    nx, ny, depth = labels.shape
    steps = states.shape[0]
    taps = [kern_x[t] for t in range(kern_x.shape[0])]
    width = (len(taps) - 1) // 2 + RIM
    tall = ny + 2 * RIM
    lo, own_rows = JOFF - RIM, slice(JOFF, JOFF + ny)
    outs = range(nx + 2 * RIM)

    def place(even):
        slab = inner.at[1 if even else 0]
        at = 0
        for k in range(width):
            ext[k, lo:lo + tall, :] = slab[pl.ds(at, tall), :]
            at += tall
        first, step = (nx + RIM, 1) if even else (RIM - 1, -1)
        for k in range(RIM):
            coef[first + step * k, lo:lo + tall, :] = slab[pl.ds(at, tall), :]
            at += tall
        kind[first, own_rows, :] = slab[pl.ds(at, ny), :]
        at += ny
        for s in range(steps):
            state[s, first, own_rows, :] = slab[pl.ds(at, ny), :]
            at += ny

    both_ways(is_even(), place)

    for x in range(nx):
        p = RIM + x
        coef[p, own_rows, :] = diffusion[x]
        kind[p, own_rows, :] = labels[x].astype(F32)
        for s in range(steps):
            state[s, p, own_rows, :] = states[s, x].astype(F32)

    def rims(first):
        left, right = (two, one) if first else (one, two)
        for x in range(nx):
            p, row = RIM + x, pl.ds(x, 1)
            for k in range(RIM):
                coef[p, lo + k:lo + k + 1, :] = left[width + k, row, :]
                coef[p, JOFF + ny + k:JOFF + ny + k + 1, :] = right[width + k, row, :]
            kind[p, JOFF - 1:JOFF, :] = left[width + RIM, row, :]
            kind[p, JOFF + ny:JOFF + ny + 1, :] = right[width + RIM, row, :]
            for s in range(steps):
                state[s, p, JOFF - 1:JOFF, :] = left[width + RIM + 1 + s, row, :]
                state[s, p, JOFF + ny:JOFF + ny + 1, :] = right[width + RIM + 1 + s, row, :]

    both_ways(right_comes_first(), rims)

    @pl.loop(0, SLOT // 8)
    def _(v):
        rows = pl.ds(pl.multiple_of(8 * v, 8), 8)

        def write(i, value):
            image[i, rows, :] = value

        def near(e):
            return blurred[pl.ds(pl.multiple_of((e - width) * SLOT + 8 * v, 8), 8), :]

        blur(near, write, taps, outs, range(width, width + nx))

        def add(even):
            here = range(width + nx, 2 * width + nx) if even else range(width)
            touched = outs[nx + 2 * RIM - width:] if even else outs[:width]
            blur(lambda e: ext[e - width - nx if even else width - 1 - e, rows, :], write, taps, touched, here,
                 base=lambda i: image[i, rows, :])

        both_ways(is_even(), add)

    last = inside(SLOT, depth)

    @pl.loop(0, nx + 2 * RIM - 1)
    def _(p):
        h = slice(0, SLOT)
        d = coef[p, h, :]
        for there, c, low, up in ((coef[p + 1, h, :], cx, xl, xu), (coef[p, 1:SLOT + 1, :], cy, yl, yu),
                                  (pltpu.roll(d, depth - 1, 1), cz, zl, zu)):
            q, r = shares(d, there)
            if c is cz:
                q, r = jnp.where(last, q, 0.0), jnp.where(last, r, 0.0)
            c[p, h, :] = 2.0 * d * q
            low[p, h, :] = 2.0 * q * q
            up[p, h, :] = 2.0 * r * r
        keep[p, h, :] = 1.0 - 0.5 * rate(kind[p, h, :], bind_t)


def last_kernel(part, coef, state, keep, cx, cy, cz, xl, xu, yl, yu, zl, zu, outer, labels, kern_x, bind_t, release_t,
                grad_h, adjoint_h, ext, image, adj, rim, grad, adjoint, sems):
    nx, ny, depth = labels.shape
    steps = state.shape[0]
    taps = [kern_x[t] for t in range(kern_x.shape[0])]
    width = (len(taps) - 1) // 2 + RIM
    tall = ny + 2 * RIM
    lo, own_rows = JOFF - RIM, slice(JOFF, JOFF + ny)
    outs = range(nx + 2 * RIM)
    even = is_even()

    for k in range(width):
        ext[k, lo:lo + tall, :] = outer[pl.ds(k * tall, tall), :]
    for k in range(RIM):
        rim[k, lo:lo + tall, :] = outer[pl.ds((width + k) * tall, tall), :]
    tail = (width + RIM) * tall
    rim[RIM, own_rows, :] = outer[pl.ds(tail, ny), :]
    for s in range(steps):
        rim[RIM + 1 + s, own_rows, :] = outer[pl.ds(tail + (1 + s) * ny, ny), :]

    @pl.loop(0, SLOT // 8)
    def _(v):
        rows = pl.ds(pl.multiple_of(8 * v, 8), 8)

        def write(i, value):
            image[i, rows, :] = value

        def add(even):
            far = range(width) if even else range(width + nx, 2 * width + nx)
            touched = outs[:width] if even else outs[nx + 2 * RIM - width:]
            blur(lambda e: ext[width - 1 - e if even else e - width - nx, rows, :], write, taps, touched, far,
                 base=lambda i: part[i, rows, :])
            for i in outs:
                if i not in touched:
                    image[i, rows, :] = part[i, rows, :]

        both_ways(even, add)

    h = slice(JOFF - RIM, JOFF - RIM + SLOT)
    down = slice(h.start - 1, h.stop - 1)
    after = slice(h.start + 1, h.stop + 1)

    def first(p, c_low, c_up, c_y, c_y_low, c_z, kept):
        a = image[p, h, :]
        total = c_up * (image[p + 1, h, :] - a) + c_low * (image[p - 1, h, :] - a)
        total += c_y * (image[p, after, :] - a) + c_y_low * (image[p, down, :] - a)
        fz = c_z * (pltpu.roll(a, depth - 1, 1) - a)
        adj[p, h, :] = kept * a + total + (fz - pltpu.roll(fz, 1, 1))

    def coupling(here, there):
        q, _ = shares(here, there)
        return 2.0 * here * q

    before, next_ = slice(JOFF - 1, JOFF - 1 + ny), slice(JOFF + 1, JOFF + 1 + ny)

    def second(p, c_low, s_low, state_low, c_up, s_up, state_up):
        at = own_rows
        a1, a0 = image[p, at, :], adj[p, at, :]
        s1, s0 = state[steps - 1, p, at, :], state[0, p, at, :]
        total, slopes = 0.0, 0.0

        def face(c, s, i, rows, states):
            change1, change0 = image[i, rows, :] - a1, adj[i, rows, :] - a0
            return c * change0, s * ((states[0] - s1) * change1 + (states[1] - s0) * change0)

        x = p - RIM
        for f, g in (face(c_low, s_low, p - 1, at, state_low), face(c_up, s_up, p + 1, at, state_up),
                     face(cy[p, before, :], yu[p, before, :], p, before,
                          (state[steps - 1, p, before, :], state[0, p, before, :])),
                     face(cy[p, at, :], yl[p, at, :], p, next_, (state[steps - 1, p, next_, :], state[0, p, next_, :]))):
            total, slopes = total + f, slopes + g
        nxt = functools.partial(pltpu.roll, shift=depth - 1, axis=1)
        change1, change0 = nxt(a1) - a1, nxt(a0) - a0
        both = (nxt(s1) - s1) * change1 + (nxt(s0) - s0) * change0
        fz = cz[p, at, :] * change0
        total += fz - pltpu.roll(fz, 1, 1)
        slopes += zl[p, at, :] * both + pltpu.roll(zu[p, at, :] * both, 1, 1)
        code = labels[x]
        bind, release = rate(code, bind_t), rate(code, release_t)
        b1 = 0.5 * a1 + release * (a1 - 0.5 * a1)
        grad[x] = -slopes
        adjoint[0, x] = a0 + total + bind * (b1 - a0)
        adjoint[1, x] = b1 + release * (a0 - b1)

    def send(n, x, count):
        at = pl.ds(x, count)
        pairs = ((grad.at[at], grad_h.at[at]), (adjoint.at[0, at], adjoint_h.at[0, at]),
                 (adjoint.at[1, at], adjoint_h.at[1, at]))
        return [pltpu.make_async_copy(a, b, sems.at[n, m]) for m, (a, b) in enumerate(pairs)]

    def near_rim(even):
        near, far, tile = (1, 0, RIM) if even else (nx + RIM, nx + RIM + 1, nx + RIM - 1)
        d, d_far, d_tile = rim[0, h, :], rim[1, h, :], coef[tile, h, :]
        c_tile, c_far = coupling(d, d_tile), coupling(d, d_far)
        c_z = jnp.where(inside(SLOT, depth), coupling(d, pltpu.roll(d, depth - 1, 1)), 0.0)
        kept = 1.0 - 0.5 * rate(rim[RIM, h, :], bind_t)
        c_low, c_up = (c_far, c_tile) if even else (c_tile, c_far)
        first(near, c_low, c_up, coupling(d, rim[0, after, :]), coupling(d, rim[0, down, :]), c_z, kept)
        inner_face = cx[tile, h, :] if even else cx[tile - 1, h, :]
        c_low, c_up = (c_tile, inner_face) if even else (inner_face, c_tile)
        first(tile, c_low, c_up, cy[tile, h, :], cy[tile, down, :], cz[tile, h, :], keep[tile, h, :])

    def near_rim_second(even):
        tile = RIM if even else nx + RIM - 1
        at = own_rows
        q, r = shares(coef[tile, at, :], rim[0, at, :])
        far = (2.0 * coef[tile, at, :] * q, 2.0 * q * q, (rim[RIM + steps, at, :], rim[RIM + 1, at, :]))
        if even:
            second(tile, *far, cx[tile, at, :], xl[tile, at, :],
                   (state[steps - 1, tile + 1, at, :], state[0, tile + 1, at, :]))
        else:
            second(tile, cx[tile - 1, at, :], xu[tile - 1, at, :],
                   (state[steps - 1, tile - 1, at, :], state[0, tile - 1, at, :]), *far)

    both_ways(even, near_rim)

    @pl.loop(0, nx)
    def _(n):
        p = n + jnp.where(even, RIM + 1, 1)
        first(p, cx[p - 1, h, :], cx[p, h, :], cy[p, h, :], cy[p, down, :], cz[p, h, :], keep[p, h, :])

    both_ways(even, near_rim_second)
    copies = send(0, jnp.where(even, 0, nx - 1), 1)
    for c in copies:
        c.start()
    base = jnp.where(even, RIM + 1, RIM)
    size = -(-(nx - 1) // 3)
    for n in range(3):
        count = min(size, nx - 1 - n * size)

        @pl.loop(n * size, n * size + count)
        def _(k):
            p = base + k
            at = own_rows
            second(p, cx[p - 1, at, :], xu[p - 1, at, :], (state[steps - 1, p - 1, at, :], state[0, p - 1, at, :]),
                   cx[p, at, :], xl[p, at, :], (state[steps - 1, p + 1, at, :], state[0, p + 1, at, :]))

        more = send(n + 1, base - RIM + n * size, count)
        for c in more:
            c.start()
        copies += more
    for c in copies:
        c.wait()


def swap_along_gy(shape, parity):
    nx, ny = shape
    pairs = []
    for i in range(nx):
        for j in range((parity + i) % 2, ny - 1, 2):
            a, b = i * ny + j, i * ny + j + 1
            pairs += [(a, b), (b, a)]
    return pairs


def shards(misfit, bleach_mask, labels, diffusion, bind_table, release_table, kern_x, kern_y, kern_z, free_states):
    nx, ny, depth = misfit.shape
    steps = free_states.shape[0]
    reach = (kern_x.shape[0] - 1) // 2
    width = reach + RIM
    tall = ny + 2 * RIM
    shape = (lax.axis_size("gx"), lax.axis_size("gy"))
    vmem = pl.BlockSpec(memory_space=pltpu.VMEM)
    smem = pl.BlockSpec(memory_space=pltpu.SMEM)
    hbm = pl.BlockSpec(memory_space=pl.ANY)
    params = pltpu.CompilerParams(vmem_limit_bytes=24 * 1024 * 1024)
    flat = (nx * ny, depth)
    array = jax.ShapeDtypeStruct

    def in_hbm(x):
        return pltpu.with_memory_space_constraint(x, pltpu.MemorySpace.HBM)

    slots = width + RIM + 1 + steps
    slab = array((slots, nx, depth), F32)
    own, one, two = pl.pallas_call(
        functools.partial(first_kernel, reach),
        out_shape=[array((ny, nx, depth), F32), slab, slab],
        in_specs=[hbm] * 6,
        out_specs=[vmem] * 3,
        scratch_shapes=[
            pltpu.VMEM(flat, F32), pltpu.VMEM(flat, jnp.int32), pltpu.VMEM(flat, jnp.int32), pltpu.VMEM(flat, F32),
            pltpu.VMEM(free_states.shape, free_states.dtype), pltpu.SMEM(kern_z.shape, F32),
            pltpu.VMEM(flat, F32), pltpu.VMEM((steps * nx * ny, depth), F32), pltpu.SemaphoreType.DMA((6,))],
        compiler_params=params,
        name="weigh_blur_z",
    )(in_hbm(misfit.reshape(flat)), in_hbm(bleach_mask.reshape(flat)), in_hbm(labels.reshape(flat)),
      in_hbm(diffusion.reshape(flat)), in_hbm(free_states), in_hbm(kern_z))
    one = lax.ppermute(one, AXES, swap_along_gy(shape, 0))
    two = lax.ppermute(two, AXES, swap_along_gy(shape, 1))

    part = pl.pallas_call(
        own_y_kernel,
        out_shape=array((tall, nx, depth), F32),
        in_specs=[vmem, smem],
        out_specs=vmem,
        compiler_params=params,
        cost_estimate=pl.CostEstimate(flops=4_000_000, bytes_accessed=700_000, transcendentals=0),
        name="own_y",
    )(own, kern_y)

    rows = (width + RIM) * tall + (1 + steps) * ny
    slab = array((rows, depth), F32)
    blurred, outer, inner = pl.pallas_call(
        rest_y_kernel,
        out_shape=[array((nx * SLOT, depth), F32), slab, slab],
        in_specs=[vmem] * 6 + [smem],
        out_specs=[vmem] * 3,
        scratch_shapes=[pltpu.VMEM((slots, nx, depth), F32)] * 2,
        compiler_params=params,
        name="rest_y",
    )(part, one, two, labels, diffusion, free_states, kern_y)

    line = shape[1]
    across = []
    for i in range(1, shape[0] - 1, 2):
        for j in range(line):
            a, b = i * line + j, (i + 1) * line + j
            across += [(a, b), (b, a)]
    within = [[i * line + j, (i + 1) * line + j] for i in range(0, shape[0], 2) for j in range(line)]
    outer = lax.ppermute(outer, AXES, across)
    inner = lax.all_gather(inner, AXES, axis_index_groups=within)

    around = (nx + 2 * RIM, HIGH, depth)
    field = array(around, F32)
    early = pl.pallas_call(
        early_x_kernel,
        out_shape=[field, field, array((steps, *around), F32)] + [field] * 10,
        in_specs=[vmem] * 7 + [smem] * 2,
        out_specs=[vmem] * 13,
        scratch_shapes=[pltpu.VMEM((width, SLOT, depth), F32), pltpu.VMEM(around, F32)],
        compiler_params=params,
        cost_estimate=pl.CostEstimate(flops=8_000_000, bytes_accessed=3_000_000, transcendentals=0),
        name="early_x",
    )(blurred, inner, one, two, labels, diffusion, free_states, kern_x, bind_table)

    tile = (nx, ny, depth)
    grad, adjoint = pl.pallas_call(
        last_kernel,
        out_shape=[array(tile, F32), array((2, *tile), F32)],
        in_specs=[vmem] * 15 + [smem] * 3,
        out_specs=[hbm] * 2,
        scratch_shapes=[
            pltpu.VMEM((width, SLOT, depth), F32),
            pltpu.VMEM(around, F32),
            pltpu.VMEM(around, F32),
            pltpu.VMEM((RIM + 1 + steps, HIGH, depth), F32),
            pltpu.VMEM(tile, F32),
            pltpu.VMEM((2, *tile), F32),
            pltpu.SemaphoreType.DMA((4, 3)),
        ],
        compiler_params=params,
        name="late_x_steps",
    )(*early, outer, labels, kern_x, bind_table, release_table)
    return grad, adjoint


def solution(mesh):
    tile = P("gx", "gy", None)
    in_specs = (tile, tile, tile, tile, P(), P(), P(), P(), P(), P(None, "gx", "gy", None))
    out_specs = (tile, P(None, "gx", "gy", None))
    return jax.shard_map(shards, mesh=mesh, in_specs=in_specs, out_specs=out_specs, check_vma=False)
```

time: 43.9 us -> 38.9 us (0.89)
  local copies, waits for them, and re-layouts: 5.48 us -> 0.03 us
  Pallas kernels: 12.8 us -> 16.6 us
  waiting for transfers between devices: 7.29 us -> 3.91 us
    unnamed x26 -> x14, local copies, waits for them, and re-layouts: 5.48 us -> 0.03 us
    pallas_call x3 -> x5, Pallas kernels: 12.8 us -> 16.7 us  [the longest x1 9 us: shards(): pl.pallas_call(last_kernel, out_shape=[array(tile, F32), array((2, *tile)...]
    ppermute x1, waiting for transfers between devices: 2.31 us -> 0.01 us  [shards(): outer = lax.ppermute(outer, AXES, across)]
    ppermute x1, waiting for transfers between devices: 4.26 us -> 3.19 us  [shards(): one = lax.ppermute(one, AXES, swap_along_gy(shape, 0))]
  transfers between devices with their start and end apart: 3 -> 3, of which waited for: 3 -> 2; matrix products, arithmetic and copies ran while one was open for 0% -> 0% of each run, Pallas kernels for 0% -> 13%
where the time goes in v2:
time: 38.9 us; the launch traced here: 38.7 us
  Pallas kernels  16.6 us (43%)
  starting transfers between devices  15.1 us (39%)
  waiting for transfers between devices  3.91 us (10%)
  blocking collectives  2.25 us (6%)
  between operations  0.76 us (2%)
    pallas_call x1, Pallas kernels, shards(): pl.pallas_call(last_kernel, out_shape=[array(tile, F32), array((2, *tile)...  9 us
    ppermute x1, starting transfers between devices, shards(): outer = lax.ppermute(outer, AXES, across)  8.83 us
    pallas_call x1, Pallas kernels, shards(): pl.pallas_call(early_x_kernel, out_shape=[field, field, array((steps, *ar...  3.93 us
    ppermute x1, starting transfers between devices, shards(): one = lax.ppermute(one, AXES, swap_along_gy(shape, 0))  3.48 us
    ppermute x1, waiting for transfers between devices, shards(): one = lax.ppermute(one, AXES, swap_along_gy(shape, 0))  3.19 us
    ppermute x1, starting transfers between devices, shards(): two = lax.ppermute(two, AXES, swap_along_gy(shape, 1))  2.76 us
    all_gather x1, blocking collectives, shards(): inner = lax.all_gather(inner, AXES, axis_index_groups=within)  2.25 us
    pallas_call x1, Pallas kernels, shards(): pl.pallas_call(functools.partial(first_kernel, reach), out_shape=[array((...  1.71 us
  transfers between devices with their start and end apart: 3, of which 2 were waited for; matrix products, arithmetic and copies ran while one was open for 0% of the time, Pallas kernels for 13%

profile of v2, /device:TPU:281, one launch (start us, length us, event | category | flops | bytes accessed | tf_op | source)
XLA Modules:
  0.0 38.7 jit_solution(7859090764013058741)
XLA Ops:
  0.6 0.0 copy-start.2
  0.6 0.0 copy-start.1
  0.7 0.0 copy-start
  0.7 0.0 copy-start.5
  0.7 1.7 %weigh_blur_z.1 = (f32[24,24,128]{2,1,0:T(8,128)S(1)}, f32[22,24,128]{2,1,0:T(8,128)S(1)}, f32[22,24,128]{2,1,0:T(8,128)S(1)}) custom-call(f32[576,128]{1,0:T(8,128)} %bitcast.8, s32[576,128]{1,0:T(8,128)} %bitcast.9, s32[576,128]{1,0:T(8,128)} %bitcast.5, f32[576,128]{1,0:T(8,128)} %bitcast.6, bf16[2,24,24,128]{3,2,1,0:T(8,128)(2,1)} %states.3, f32[63]{0:T(128)} %kern_h.1), custom_call_target="tpu_custom_call" | custom-call | tf_op jit(solution)/shard_map/weigh_blur_z/pallas_call | solution.py:443
  2.4 3.5 %collective-permute-start = (f32[22,24,128]{2,1,0:T(8,128)S(1)}, f32[22,24,128]{2,1,0:T(8,128)S(1)}, u32[]{:S(2)}, u32[]{:S(2)}) collective-permute-start(f32[22,24,128]{2,1,0:T(8,128)S(1)} %get-tuple-element.22), channel_id=1, source_target_pairs={{0,1},{1,0},{2,3},{3,2},{4,5},{5,4},{6,7},{7,6},{8,9},{9,8},{10,11... | collective-permute-start | bytes 811016 | tf_op jit(solution)/shard_map/ppermute | solution.py:456
  5.9 2.8 %collective-permute-start.1 = (f32[22,24,128]{2,1,0:T(8,128)S(1)}, f32[22,24,128]{2,1,0:T(8,128)S(1)}, u32[]{:S(2)}, u32[]{:S(2)}) collective-permute-start(f32[22,24,128]{2,1,0:T(8,128)S(1)} %get-tuple-element.23), channel_id=1, source_target_pairs={{1,2},{2,1},{3,4},{4,3},{5,6},{6,5},{7,8},{8,7},{9,10},{10,9},{11,... | collective-permute-start | bytes 811016 | tf_op jit(solution)/shard_map/ppermute | solution.py:457
  8.6 0.0 copy-done.5
  8.7 1.0 %own_y.1.part = f32[28,24,128]{2,1,0:T(8,128)S(1)} custom-call(f32[24,24,128]{2,1,0:T(8,128)S(1)} %get-tuple-element.21.own, f32[31]{0:T(128)S(1)} %copy-done.5), custom_call_target="tpu_custom_call" | custom-call | flops 4000000 | bytes 700000 | tf_op jit(solution)/shard_map/own_y/pallas_call | solution.py:459
  9.7 0.0 copy-start.3
  9.7 0.0 copy-start.4
  9.7 3.2 %collective-permute-done.one = f32[22,24,128]{2,1,0:T(8,128)S(1)} collective-permute-done((f32[22,24,128]{2,1,0:T(8,128)S(1)}, f32[22,24,128]{2,1,0:T(8,128)S(1)}, u32[]{:S(2)}, u32[]{:S(2)}) %collective-permute-start) | collective-permute-done | bytes 270368 | tf_op jit(solution)/shard_map/ppermute | solution.py:456
  12.9 0.7 %collective-permute-done.1.two = f32[22,24,128]{2,1,0:T(8,128)S(1)} collective-permute-done((f32[22,24,128]{2,1,0:T(8,128)S(1)}, f32[22,24,128]{2,1,0:T(8,128)S(1)}, u32[]{:S(2)}, u32[]{:S(2)}) %collective-permute-start.1) | collective-permute-done | bytes 270368 | tf_op jit(solution)/shard_map/ppermute | solution.py:457
  13.6 0.0 copy-done.2
  13.6 0.0 copy-done.1
  13.6 0.0 copy-done
  13.6 1.0 %rest_y.1 = (f32[768,128]{1,0:T(8,128)S(1)}, f32[604,128]{1,0:T(8,128)S(1)}, f32[604,128]{1,0:T(8,128)S(1)}) custom-call(f32[28,24,128]{2,1,0:T(8,128)S(1)} %own_y.1.part, f32[22,24,128]{2,1,0:T(8,128)S(1)} %collective-permute-done.one, f32[22,24,128]{2,1,0:T(8,128)S(1)} %collective-permute-done.1.two, s32[24,24,128]{2,1,0:T(8,128)S(1)} %copy-done, ...), custom_call_target="tpu_custom_call" | custom-call | tf_op jit(solution)/shard_map/rest_y/pallas_call | solution.py:471
  14.6 8.8 %collective-permute-start.2 = (f32[604,128]{1,0:T(8,128)S(1)}, f32[604,128]{1,0:T(8,128)S(1)}, u32[]{:S(2)}, u32[]{:S(2)}) collective-permute-start(f32[604,128]{1,0:T(8,128)S(1)} %get-tuple-element.39), channel_id=1, source_target_pairs={{32,64},{64,32},{33,65},{65,33},{34,66},{66,34},{35,67},{67,35},{3... | collective-permute-start | bytes 927752 | tf_op jit(solution)/shard_map/ppermute | solution.py:488
  23.5 2.3 %all-gather.1.inner = f32[2,604,128]{2,1,0:T(8,128)S(1)} all-gather(f32[1,604,128]{2,1,0:T(8,128)S(1)} %bitcast.7), channel_id=2, replica_groups={{0,32},{1,33},{2,34},{3,35},{4,36},{5,37},{6,38},{7,39},{8,40},{9,41},{..., dimensions={0}, use_global_device_ids=true | all-gather | bytes 927744 | tf_op jit(solution)/shard_map/all_gather | solution.py:489
  25.7 0.0 copy-done.3
  25.7 0.0 copy-done.4
  25.7 0.0 copy-start.6
  25.7 3.9 %early_x.1 = (f32[28,40,128]{2,1,0:T(8,128)S(1)}, f32[28,40,128]{2,1,0:T(8,128)S(1)}, f32[2,28,40,128]{3,2,1,0:T(8,128)S(1)}, f32[28,40,128]{2,1,0:T(8,128)S(1)}...) custom-call(f32[768,128]{1,0:T(8,128)S(1)} %get-tuple-element.24.blu, ...), custom_call_target="tpu_custom_call" | custom-call | flops 8000000 | bytes 3000000 | tf_op jit(solution)/shard_map/early_x/pallas_call | solution.py:493
  29.6 0.0 collective-permute-done.2.outer
  29.7 0.0 copy-done.6
  29.7 9.0 %late_x_steps.1 = (f32[24,24,128]{2,1,0:T(8,128)}, f32[2,24,24,128]{3,2,1,0:T(8,128)}) custom-call(f32[28,40,128]{2,1,0:T(8,128)S(1)} %get-tuple-element.26.part, f32[28,40,128]{2,1,0:T(8,128)S(1)} %get-tuple-element.27.coef, f32[2,28,40,128]{3,2,1,0:T(8,128)S(1)} %get-tuple-element.28.state, f32[28,40,128]{2,1,0:T(8,128)S(1)} %get-tuple-element.29.keep, ...), custom_call_target="tpu_custom_call" | custom-call | tf_op jit(solution)/shard_map/late_x_steps/pallas_call | solution.py:505
Async XLA Ops:
  0.6 13.0 %copy-start.2 = (bf16[2,24,24,128]{3,2,1,0:T(8,128)(2,1)S(1)}, bf16[2,24,24,128]{3,2,1,0:T(8,128)(2,1)}, u32[]{:S(2)}) copy-start(bf16[2,24,24,128]{3,2,1,0:T(8,128)(2,1)} %states.3) | copy-start | bytes 884740
  0.6 13.0 %copy-start.1 = (f32[24,24,128]{2,1,0:T(8,128)S(1)}, f32[24,24,128]{2,1,0:T(8,128)}, u32[]{:S(2)}) copy-start(f32[24,24,128]{2,1,0:T(8,128)} %diffusion.3) | copy-start | bytes 884740
  0.7 13.0 %copy-start = (s32[24,24,128]{2,1,0:T(8,128)S(1)}, s32[24,24,128]{2,1,0:T(8,128)}, u32[]{:S(2)}) copy-start(s32[24,24,128]{2,1,0:T(8,128)} %labels.5) | copy-start | bytes 884740
  0.7 8.0 %copy-start.5 = (f32[31]{0:T(128)S(1)}, f32[31]{0:T(128)}, u32[]{:S(2)}) copy-start(f32[31]{0:T(128)} %kern_y.3) | copy-start | bytes 376
  2.4 10.5 %collective-permute-start = (f32[22,24,128]{2,1,0:T(8,128)S(1)}, f32[22,24,128]{2,1,0:T(8,128)S(1)}, u32[]{:S(2)}, u32[]{:S(2)}) collective-permute-start(f32[22,24,128]{2,1,0:T(8,128)S(1)} %get-tuple-element.22), channel_id=1, source_target_pairs={{0,1},{1,0},{2,3},{3,2},{4,5},{5,4},{6,7},{7,6},{8,9},{9,8},{10,11... | collective-permute-start | bytes 811016 | tf_op jit(solution)/shard_map/ppermute | solution.py:456
  5.9 7.7 %collective-permute-start.1 = (f32[22,24,128]{2,1,0:T(8,128)S(1)}, f32[22,24,128]{2,1,0:T(8,128)S(1)}, u32[]{:S(2)}, u32[]{:S(2)}) collective-permute-start(f32[22,24,128]{2,1,0:T(8,128)S(1)} %get-tuple-element.23), channel_id=1, source_target_pairs={{1,2},{2,1},{3,4},{4,3},{5,6},{6,5},{7,8},{8,7},{9,10},{10,9},{11,... | collective-permute-start | bytes 811016 | tf_op jit(solution)/shard_map/ppermute | solution.py:457
  9.7 16.0 %copy-start.3 = (f32[31]{0:T(128)S(1)}, f32[31]{0:T(128)}, u32[]{:S(2)}) copy-start(f32[31]{0:T(128)} %kern_x.3) | copy-start | bytes 376
  9.7 16.0 %copy-start.4 = (f32[3]{0:T(128)S(1)}, f32[3]{0:T(128)}, u32[]{:S(2)}) copy-start(f32[3]{0:T(128)} %bind_t.3) | copy-start | bytes 40
  14.6 15.0 %collective-permute-start.2 = (f32[604,128]{1,0:T(8,128)S(1)}, f32[604,128]{1,0:T(8,128)S(1)}, u32[]{:S(2)}, u32[]{:S(2)}) collective-permute-start(f32[604,128]{1,0:T(8,128)S(1)} %get-tuple-element.39), channel_id=1, source_target_pairs={{32,64},{64,32},{33,65},{65,33},{34,66},{66,34},{35,67},{67,35},{3... | collective-permute-start | bytes 927752 | tf_op jit(solution)/shard_map/ppermute | solution.py:488
  25.7 3.9 %copy-start.6 = (f32[3]{0:T(128)S(1)}, f32[3]{0:T(128)}, u32[]{:S(2)}) copy-start(f32[3]{0:T(128)} %release_t.1) | copy-start | bytes 40

commit v3 on v2

--- a/solution.py
+++ b/solution.py
@@ -12,6 +12,7 @@
 JOFF = 4
 SLOT = 32
 HIGH = 40
+CHUNKS = 4
 F32 = jnp.float32
 
 
@@ -251,7 +252,7 @@
 
     last = inside(SLOT, depth)
 
-    @pl.loop(0, nx + 2 * RIM - 1)
+    @pl.loop(0, nx + 2 * RIM - 1, unroll=9)
     def _(p):
         h = slice(0, SLOT)
         d = coef[p, h, :]
@@ -382,7 +383,7 @@
 
     both_ways(even, near_rim)
 
-    @pl.loop(0, nx)
+    @pl.loop(0, nx, unroll=8)
     def _(n):
         p = n + jnp.where(even, RIM + 1, 1)
         first(p, cx[p - 1, h, :], cx[p, h, :], cy[p, h, :], cy[p, down, :], cz[p, h, :], keep[p, h, :])
@@ -392,11 +393,11 @@
     for c in copies:
         c.start()
     base = jnp.where(even, RIM + 1, RIM)
-    size = -(-(nx - 1) // 3)
-    for n in range(3):
+    size = -(-(nx - 1) // CHUNKS)
+    for n in range(CHUNKS):
         count = min(size, nx - 1 - n * size)
 
-        @pl.loop(n * size, n * size + count)
+        @pl.loop(n * size, n * size + count, unroll=count)
         def _(k):
             p = base + k
             at = own_rows
@@ -514,7 +515,7 @@
             pltpu.VMEM((RIM + 1 + steps, HIGH, depth), F32),
             pltpu.VMEM(tile, F32),
             pltpu.VMEM((2, *tile), F32),
-            pltpu.SemaphoreType.DMA((4, 3)),
+            pltpu.SemaphoreType.DMA((CHUNKS + 1, 3)),
         ],
         compiler_params=params,
         name="late_x_steps",

time: 38.9 us -> 32.5 us (0.84)
  Pallas kernels: 16.6 us -> 10.3 us
    pallas_call x1, Pallas kernels: 9 us -> 4.33 us  [shards(): pl.pallas_call(last_kernel, out_shape=[array(tile, F32), array((2, *tile)...]
    pallas_call x1, Pallas kernels: 3.93 us -> 2.29 us  [shards(): pl.pallas_call(early_x_kernel, out_shape=[field, field, array((steps, *ar...]
  transfers between devices with their start and end apart: 3 -> 3, of which waited for: 2 -> 2; matrix products, arithmetic and copies ran while one was open for 0% -> 0% of each run, Pallas kernels for 13% -> 10%
where the time goes in v3:
time: 32.5 us; the launch traced here: 32.4 us
  starting transfers between devices  15.1 us (46%)
  Pallas kernels  10.3 us (32%)
  waiting for transfers between devices  3.92 us (12%)
  blocking collectives  2.25 us (7%)
  between operations  0.75 us (2%)
    ppermute x1, starting transfers between devices, shards(): outer = lax.ppermute(outer, AXES, across)  8.83 us
    pallas_call x1, Pallas kernels, shards(): pl.pallas_call(last_kernel, out_shape=[array(tile, F32), array((2, *tile)...  4.33 us
    ppermute x1, starting transfers between devices, shards(): one = lax.ppermute(one, AXES, swap_along_gy(shape, 0))  3.48 us
    ppermute x1, waiting for transfers between devices, shards(): one = lax.ppermute(one, AXES, swap_along_gy(shape, 0))  3.19 us
    ppermute x1, starting transfers between devices, shards(): two = lax.ppermute(two, AXES, swap_along_gy(shape, 1))  2.76 us
    pallas_call x1, Pallas kernels, shards(): pl.pallas_call(early_x_kernel, out_shape=[field, field, array((steps, *ar...  2.29 us
    all_gather x1, blocking collectives, shards(): inner = lax.all_gather(inner, AXES, axis_index_groups=within)  2.25 us
    pallas_call x1, Pallas kernels, shards(): pl.pallas_call(functools.partial(first_kernel, reach), out_shape=[array((...  1.71 us
  transfers between devices with their start and end apart: 3, of which 2 were waited for; matrix products, arithmetic and copies ran while one was open for 0% of the time, Pallas kernels for 10%

profile of v3, /device:TPU:281, one launch (start us, length us, event | category | flops | bytes accessed | tf_op | source)
XLA Modules:
  0.0 32.4 jit_solution(14877020923513085839)
XLA Ops:
  0.6 0.0 copy-start.2
  0.6 0.0 copy-start.1
  0.7 0.0 copy-start
  0.7 0.0 copy-start.5
  0.7 1.7 %weigh_blur_z.1 = (f32[24,24,128]{2,1,0:T(8,128)S(1)}, f32[22,24,128]{2,1,0:T(8,128)S(1)}, f32[22,24,128]{2,1,0:T(8,128)S(1)}) custom-call(f32[576,128]{1,0:T(8,128)} %bitcast.8, s32[576,128]{1,0:T(8,128)} %bitcast.9, s32[576,128]{1,0:T(8,128)} %bitcast.5, f32[576,128]{1,0:T(8,128)} %bitcast.6, bf16[2,24,24,128]{3,2,1,0:T(8,128)(2,1)} %states.3, f32[63]{0:T(128)} %kern_h.1), custom_call_target="tpu_custom_call" | custom-call | tf_op jit(solution)/shard_map/weigh_blur_z/pallas_call | solution.py:444
  2.4 3.5 %collective-permute-start = (f32[22,24,128]{2,1,0:T(8,128)S(1)}, f32[22,24,128]{2,1,0:T(8,128)S(1)}, u32[]{:S(2)}, u32[]{:S(2)}) collective-permute-start(f32[22,24,128]{2,1,0:T(8,128)S(1)} %get-tuple-element.22), channel_id=1, source_target_pairs={{0,1},{1,0},{2,3},{3,2},{4,5},{5,4},{6,7},{7,6},{8,9},{9,8},{10,11... | collective-permute-start | bytes 811016 | tf_op jit(solution)/shard_map/ppermute | solution.py:457
  5.9 2.8 %collective-permute-start.1 = (f32[22,24,128]{2,1,0:T(8,128)S(1)}, f32[22,24,128]{2,1,0:T(8,128)S(1)}, u32[]{:S(2)}, u32[]{:S(2)}) collective-permute-start(f32[22,24,128]{2,1,0:T(8,128)S(1)} %get-tuple-element.23), channel_id=1, source_target_pairs={{1,2},{2,1},{3,4},{4,3},{5,6},{6,5},{7,8},{8,7},{9,10},{10,9},{11,... | collective-permute-start | bytes 811016 | tf_op jit(solution)/shard_map/ppermute | solution.py:458
  8.6 0.0 copy-done.5
  8.7 1.0 %own_y.1.part = f32[28,24,128]{2,1,0:T(8,128)S(1)} custom-call(f32[24,24,128]{2,1,0:T(8,128)S(1)} %get-tuple-element.21.own, f32[31]{0:T(128)S(1)} %copy-done.5), custom_call_target="tpu_custom_call" | custom-call | flops 4000000 | bytes 700000 | tf_op jit(solution)/shard_map/own_y/pallas_call | solution.py:460
  9.7 0.0 copy-start.3
  9.7 0.0 copy-start.4
  9.7 3.2 %collective-permute-done.one = f32[22,24,128]{2,1,0:T(8,128)S(1)} collective-permute-done((f32[22,24,128]{2,1,0:T(8,128)S(1)}, f32[22,24,128]{2,1,0:T(8,128)S(1)}, u32[]{:S(2)}, u32[]{:S(2)}) %collective-permute-start) | collective-permute-done | bytes 270368 | tf_op jit(solution)/shard_map/ppermute | solution.py:457
  12.9 0.7 %collective-permute-done.1.two = f32[22,24,128]{2,1,0:T(8,128)S(1)} collective-permute-done((f32[22,24,128]{2,1,0:T(8,128)S(1)}, f32[22,24,128]{2,1,0:T(8,128)S(1)}, u32[]{:S(2)}, u32[]{:S(2)}) %collective-permute-start.1) | collective-permute-done | bytes 270368 | tf_op jit(solution)/shard_map/ppermute | solution.py:458
  13.6 0.0 copy-done.2
  13.6 0.0 copy-done.1
  13.6 0.0 copy-done
  13.6 1.0 %rest_y.1 = (f32[768,128]{1,0:T(8,128)S(1)}, f32[604,128]{1,0:T(8,128)S(1)}, f32[604,128]{1,0:T(8,128)S(1)}) custom-call(f32[28,24,128]{2,1,0:T(8,128)S(1)} %own_y.1.part, f32[22,24,128]{2,1,0:T(8,128)S(1)} %collective-permute-done.one, f32[22,24,128]{2,1,0:T(8,128)S(1)} %collective-permute-done.1.two, s32[24,24,128]{2,1,0:T(8,128)S(1)} %copy-done, ...), custom_call_target="tpu_custom_call" | custom-call | tf_op jit(solution)/shard_map/rest_y/pallas_call | solution.py:472
  14.6 8.8 %collective-permute-start.2 = (f32[604,128]{1,0:T(8,128)S(1)}, f32[604,128]{1,0:T(8,128)S(1)}, u32[]{:S(2)}, u32[]{:S(2)}) collective-permute-start(f32[604,128]{1,0:T(8,128)S(1)} %get-tuple-element.39), channel_id=1, source_target_pairs={{32,64},{64,32},{33,65},{65,33},{34,66},{66,34},{35,67},{67,35},{3... | collective-permute-start | bytes 927752 | tf_op jit(solution)/shard_map/ppermute | solution.py:489
  23.5 2.3 %all-gather.1.inner = f32[2,604,128]{2,1,0:T(8,128)S(1)} all-gather(f32[1,604,128]{2,1,0:T(8,128)S(1)} %bitcast.7), channel_id=2, replica_groups={{0,32},{1,33},{2,34},{3,35},{4,36},{5,37},{6,38},{7,39},{8,40},{9,41},{..., dimensions={0}, use_global_device_ids=true | all-gather | bytes 927744 | tf_op jit(solution)/shard_map/all_gather | solution.py:490
  25.7 0.0 copy-done.3
  25.7 0.0 copy-done.4
  25.7 0.0 copy-start.6
  25.7 2.3 %early_x.1 = (f32[28,40,128]{2,1,0:T(8,128)S(1)}, f32[28,40,128]{2,1,0:T(8,128)S(1)}, f32[2,28,40,128]{3,2,1,0:T(8,128)S(1)}, f32[28,40,128]{2,1,0:T(8,128)S(1)}...) custom-call(f32[768,128]{1,0:T(8,128)S(1)} %get-tuple-element.24.blu, ...), custom_call_target="tpu_custom_call" | custom-call | flops 8000000 | bytes 3000000 | tf_op jit(solution)/shard_map/early_x/pallas_call | solution.py:494
  28.0 0.0 collective-permute-done.2.outer
  28.0 0.0 copy-done.6
  28.0 4.3 %late_x_steps.1 = (f32[24,24,128]{2,1,0:T(8,128)}, f32[2,24,24,128]{3,2,1,0:T(8,128)}) custom-call(f32[28,40,128]{2,1,0:T(8,128)S(1)} %get-tuple-element.26.part, f32[28,40,128]{2,1,0:T(8,128)S(1)} %get-tuple-element.27.coef, f32[2,28,40,128]{3,2,1,0:T(8,128)S(1)} %get-tuple-element.28.state, f32[28,40,128]{2,1,0:T(8,128)S(1)} %get-tuple-element.29.keep, ...), custom_call_target="tpu_custom_call" | custom-call | tf_op jit(solution)/shard_map/late_x_steps/pallas_call | solution.py:506
Async XLA Ops:
  0.6 13.0 %copy-start.2 = (bf16[2,24,24,128]{3,2,1,0:T(8,128)(2,1)S(1)}, bf16[2,24,24,128]{3,2,1,0:T(8,128)(2,1)}, u32[]{:S(2)}) copy-start(bf16[2,24,24,128]{3,2,1,0:T(8,128)(2,1)} %states.3) | copy-start | bytes 884740
  0.6 13.0 %copy-start.1 = (f32[24,24,128]{2,1,0:T(8,128)S(1)}, f32[24,24,128]{2,1,0:T(8,128)}, u32[]{:S(2)}) copy-start(f32[24,24,128]{2,1,0:T(8,128)} %diffusion.3) | copy-start | bytes 884740
  0.7 13.0 %copy-start = (s32[24,24,128]{2,1,0:T(8,128)S(1)}, s32[24,24,128]{2,1,0:T(8,128)}, u32[]{:S(2)}) copy-start(s32[24,24,128]{2,1,0:T(8,128)} %labels.5) | copy-start | bytes 884740
  0.7 8.0 %copy-start.5 = (f32[31]{0:T(128)S(1)}, f32[31]{0:T(128)}, u32[]{:S(2)}) copy-start(f32[31]{0:T(128)} %kern_y.3) | copy-start | bytes 376
  2.4 10.5 %collective-permute-start = (f32[22,24,128]{2,1,0:T(8,128)S(1)}, f32[22,24,128]{2,1,0:T(8,128)S(1)}, u32[]{:S(2)}, u32[]{:S(2)}) collective-permute-start(f32[22,24,128]{2,1,0:T(8,128)S(1)} %get-tuple-element.22), channel_id=1, source_target_pairs={{0,1},{1,0},{2,3},{3,2},{4,5},{5,4},{6,7},{7,6},{8,9},{9,8},{10,11... | collective-permute-start | bytes 811016 | tf_op jit(solution)/shard_map/ppermute | solution.py:457
  5.9 7.7 %collective-permute-start.1 = (f32[22,24,128]{2,1,0:T(8,128)S(1)}, f32[22,24,128]{2,1,0:T(8,128)S(1)}, u32[]{:S(2)}, u32[]{:S(2)}) collective-permute-start(f32[22,24,128]{2,1,0:T(8,128)S(1)} %get-tuple-element.23), channel_id=1, source_target_pairs={{1,2},{2,1},{3,4},{4,3},{5,6},{6,5},{7,8},{8,7},{9,10},{10,9},{11,... | collective-permute-start | bytes 811016 | tf_op jit(solution)/shard_map/ppermute | solution.py:458
  9.7 16.0 %copy-start.3 = (f32[31]{0:T(128)S(1)}, f32[31]{0:T(128)}, u32[]{:S(2)}) copy-start(f32[31]{0:T(128)} %kern_x.3) | copy-start | bytes 376
  9.7 16.0 %copy-start.4 = (f32[3]{0:T(128)S(1)}, f32[3]{0:T(128)}, u32[]{:S(2)}) copy-start(f32[3]{0:T(128)} %bind_t.3) | copy-start | bytes 40
  14.6 13.4 %collective-permute-start.2 = (f32[604,128]{1,0:T(8,128)S(1)}, f32[604,128]{1,0:T(8,128)S(1)}, u32[]{:S(2)}, u32[]{:S(2)}) collective-permute-start(f32[604,128]{1,0:T(8,128)S(1)} %get-tuple-element.39), channel_id=1, source_target_pairs={{32,64},{64,32},{33,65},{65,33},{34,66},{66,34},{35,67},{67,35},{3... | collective-permute-start | bytes 927752 | tf_op jit(solution)/shard_map/ppermute | solution.py:489
  25.7 2.3 %copy-start.6 = (f32[3]{0:T(128)S(1)}, f32[3]{0:T(128)}, u32[]{:S(2)}) copy-start(f32[3]{0:T(128)} %release_t.1) | copy-start | bytes 40

commit v4 on v3

--- a/solution.py
+++ b/solution.py
@@ -32,8 +32,15 @@
             write(i, acc[i])
 
 
+def vectors(spread, reach):
+    span = 2 * reach + 1
+    taps_x, taps_y, bind = range(span), range(span, 2 * span), 2 * span
+    kinds = (spread.shape[0] - bind) // 2
+    return taps_x, taps_y, range(bind, bind + kinds), range(bind + kinds, bind + 2 * kinds)
+
+
 def right_comes_first():
-    return (lax.axis_index("gx") + lax.axis_index("gy")) % 2 == 0
+    return (lax.axis_index("gx") + lax.axis_index("gy")) % 2 == 1
 
 
 def is_even():
@@ -45,12 +52,13 @@
     pl.when(jnp.logical_not(flag))(functools.partial(act, False))
 
 
-def first_kernel(reach, misfit_h, mask_h, labels_h, diffusion_h, states_h, kern_h, own, one, two,
-                 misfit, mask, labels, diffusion, states, kern, work, edge, sems):
+def first_kernel(reach, misfit_h, mask_h, labels_h, diffusion_h, states_h, kern_h, *rest):
+    few_h, rest = rest[:4], rest[4:]
+    own, one, two, spread, misfit, mask, labels, diffusion, states, kern, work, edge, *few, sems = rest
     steps, nx, ny, depth = states.shape
     copies = [pltpu.make_async_copy(a, b, sems.at[n]) for n, (a, b) in enumerate(
-        ((kern_h, kern), (misfit_h, misfit), (mask_h, mask), (diffusion_h, diffusion), (labels_h, labels), (states_h, states)))]
-    for c in copies:
+        ((kern_h, kern), (misfit_h, misfit), (mask_h, mask), (diffusion_h, diffusion), (labels_h, labels), (states_h, states), *zip(few_h, few)))]
+    for c in copies[:3] + copies[6:] + copies[3:6]:
         c.start()
     taps_z = kern.shape[0]
     half = (taps_z - 1) // 2
@@ -64,13 +72,20 @@
     w = lax.broadcasted_iota(jnp.int32, (depth, depth), 0)
     z = lax.broadcasted_iota(jnp.int32, (depth, depth), 1)
     matrix = jnp.where(jnp.abs(z - w) <= half, rolled, 0.0)
+    for c in copies[6:]:
+        c.wait()
+    at = 0
+    for table in few:
+        for t in range(table.shape[0]):
+            spread[at] = jnp.full((8, depth), table[t], F32)
+            at += 1
     copies[1].wait()
     copies[2].wait()
     weighted = (1.0 + 3.0 * mask[...].astype(F32)) * misfit[...]
     work[...] = lax.dot_general(
         weighted, matrix, (((1,), (1,)), ((), ())),
         precision=lax.Precision.HIGHEST, preferred_element_type=F32)
-    for c in copies[3:]:
+    for c in copies[3:6]:
         c.wait()
     edge[...] = states[...].astype(F32).reshape(edge.shape)
     octets = nx // 8
@@ -102,9 +117,9 @@
     both_ways(right_comes_first(), act)
 
 
-def own_y_kernel(own, kern_y, part):
+def own_y_kernel(reach, own, spread, part):
     ny, nx, _ = own.shape
-    taps = [kern_y[t] for t in range(kern_y.shape[0])]
+    taps = [spread[t] for t in vectors(spread, reach)[1]]
     width = (len(taps) - 1) // 2 + RIM
 
     @pl.loop(0, nx // 8)
@@ -117,10 +132,10 @@
         blur(lambda e: own[e - width, at, :], write, taps, range(ny + 2 * RIM), range(width, width + ny))
 
 
-def rest_y_kernel(part, one, two, labels, diffusion, states, kern_y, blurred, outer, inner, left, right):
+def rest_y_kernel(reach, part, one, two, labels, diffusion, states, spread, blurred, outer, inner, left, right):
     tall, nx, depth = part.shape
     ny = tall - 2 * RIM
-    taps = [kern_y[t] for t in range(kern_y.shape[0])]
+    taps = [spread[t] for t in vectors(spread, reach)[1]]
     width = (len(taps) - 1) // 2 + RIM
 
     def place(first):
@@ -180,11 +195,13 @@
     return lax.broadcasted_iota(jnp.int32, (rows, depth), 1) < depth - 1
 
 
-def early_x_kernel(blurred, inner, one, two, labels, diffusion, states, kern_x, bind_t,
+def early_x_kernel(reach, blurred, inner, one, two, labels, diffusion, states, spread,
                    image, coef, state, keep, cx, cy, cz, xl, xu, yl, yu, zl, zu, ext, kind):
     nx, ny, depth = labels.shape
     steps = states.shape[0]
-    taps = [kern_x[t] for t in range(kern_x.shape[0])]
+    taps_at, _, bind_at, _ = vectors(spread, reach)
+    taps = [spread[t] for t in taps_at]
+    bind_t = [spread[t, 0:1, :] for t in bind_at]
     width = (len(taps) - 1) // 2 + RIM
     tall = ny + 2 * RIM
     lo, own_rows = JOFF - RIM, slice(JOFF, JOFF + ny)
@@ -267,11 +284,13 @@
         keep[p, h, :] = 1.0 - 0.5 * rate(kind[p, h, :], bind_t)
 
 
-def last_kernel(part, coef, state, keep, cx, cy, cz, xl, xu, yl, yu, zl, zu, outer, labels, kern_x, bind_t, release_t,
+def last_kernel(reach, part, coef, state, keep, cx, cy, cz, xl, xu, yl, yu, zl, zu, outer, labels, spread,
                 grad_h, adjoint_h, ext, image, adj, rim, grad, adjoint, sems):
     nx, ny, depth = labels.shape
     steps = state.shape[0]
-    taps = [kern_x[t] for t in range(kern_x.shape[0])]
+    taps_at, _, bind_at, release_at = vectors(spread, reach)
+    taps = [spread[t] for t in taps_at]
+    bind_t, release_t = ([spread[t, 0:1, :] for t in at] for at in (bind_at, release_at))
     width = (len(taps) - 1) // 2 + RIM
     tall = ny + 2 * RIM
     lo, own_rows = JOFF - RIM, slice(JOFF, JOFF + ny)
@@ -416,7 +435,7 @@
     nx, ny = shape
     pairs = []
     for i in range(nx):
-        for j in range((parity + i) % 2, ny - 1, 2):
+        for j in range((parity + i + 1) % 2, ny - 1, 2):
             a, b = i * ny + j, i * ny + j + 1
             pairs += [(a, b), (b, a)]
     return pairs
@@ -430,7 +449,6 @@
     tall = ny + 2 * RIM
     shape = (lax.axis_size("gx"), lax.axis_size("gy"))
     vmem = pl.BlockSpec(memory_space=pltpu.VMEM)
-    smem = pl.BlockSpec(memory_space=pltpu.SMEM)
     hbm = pl.BlockSpec(memory_space=pl.ANY)
     params = pltpu.CompilerParams(vmem_limit_bytes=24 * 1024 * 1024)
     flat = (nx * ny, depth)
@@ -441,43 +459,45 @@
 
     slots = width + RIM + 1 + steps
     slab = array((slots, nx, depth), F32)
-    own, one, two = pl.pallas_call(
+    few = (kern_x, kern_y, bind_table, release_table)
+    own, one, two, spread = pl.pallas_call(
         functools.partial(first_kernel, reach),
-        out_shape=[array((ny, nx, depth), F32), slab, slab],
-        in_specs=[hbm] * 6,
-        out_specs=[vmem] * 3,
+        out_shape=[array((ny, nx, depth), F32), slab, slab, array((sum(t.shape[0] for t in few), 8, depth), F32)],
+        in_specs=[hbm] * (6 + len(few)),
+        out_specs=[vmem] * 4,
         scratch_shapes=[
             pltpu.VMEM(flat, F32), pltpu.VMEM(flat, jnp.int32), pltpu.VMEM(flat, jnp.int32), pltpu.VMEM(flat, F32),
             pltpu.VMEM(free_states.shape, free_states.dtype), pltpu.SMEM(kern_z.shape, F32),
-            pltpu.VMEM(flat, F32), pltpu.VMEM((steps * nx * ny, depth), F32), pltpu.SemaphoreType.DMA((6,))],
+            pltpu.VMEM(flat, F32), pltpu.VMEM((steps * nx * ny, depth), F32),
+            *(pltpu.SMEM(t.shape, F32) for t in few), pltpu.SemaphoreType.DMA((6 + len(few),))],
         compiler_params=params,
         name="weigh_blur_z",
     )(in_hbm(misfit.reshape(flat)), in_hbm(bleach_mask.reshape(flat)), in_hbm(labels.reshape(flat)),
-      in_hbm(diffusion.reshape(flat)), in_hbm(free_states), in_hbm(kern_z))
+      in_hbm(diffusion.reshape(flat)), in_hbm(free_states), in_hbm(kern_z), *map(in_hbm, few))
     one = lax.ppermute(one, AXES, swap_along_gy(shape, 0))
     two = lax.ppermute(two, AXES, swap_along_gy(shape, 1))
 
     part = pl.pallas_call(
-        own_y_kernel,
+        functools.partial(own_y_kernel, reach),
         out_shape=array((tall, nx, depth), F32),
-        in_specs=[vmem, smem],
+        in_specs=[vmem] * 2,
         out_specs=vmem,
         compiler_params=params,
         cost_estimate=pl.CostEstimate(flops=4_000_000, bytes_accessed=700_000, transcendentals=0),
         name="own_y",
-    )(own, kern_y)
+    )(own, spread)
 
     rows = (width + RIM) * tall + (1 + steps) * ny
     slab = array((rows, depth), F32)
     blurred, outer, inner = pl.pallas_call(
-        rest_y_kernel,
+        functools.partial(rest_y_kernel, reach),
         out_shape=[array((nx * SLOT, depth), F32), slab, slab],
-        in_specs=[vmem] * 6 + [smem],
+        in_specs=[vmem] * 7,
         out_specs=[vmem] * 3,
         scratch_shapes=[pltpu.VMEM((slots, nx, depth), F32)] * 2,
         compiler_params=params,
         name="rest_y",
-    )(part, one, two, labels, diffusion, free_states, kern_y)
+    )(part, one, two, labels, diffusion, free_states, spread)
 
     line = shape[1]
     across = []
@@ -492,21 +512,21 @@
     around = (nx + 2 * RIM, HIGH, depth)
     field = array(around, F32)
     early = pl.pallas_call(
-        early_x_kernel,
+        functools.partial(early_x_kernel, reach),
         out_shape=[field, field, array((steps, *around), F32)] + [field] * 10,
-        in_specs=[vmem] * 7 + [smem] * 2,
+        in_specs=[vmem] * 8,
         out_specs=[vmem] * 13,
         scratch_shapes=[pltpu.VMEM((width, SLOT, depth), F32), pltpu.VMEM(around, F32)],
         compiler_params=params,
         cost_estimate=pl.CostEstimate(flops=8_000_000, bytes_accessed=3_000_000, transcendentals=0),
         name="early_x",
-    )(blurred, inner, one, two, labels, diffusion, free_states, kern_x, bind_table)
+    )(blurred, inner, one, two, labels, diffusion, free_states, spread)
 
     tile = (nx, ny, depth)
     grad, adjoint = pl.pallas_call(
-        last_kernel,
+        functools.partial(last_kernel, reach),
         out_shape=[array(tile, F32), array((2, *tile), F32)],
-        in_specs=[vmem] * 15 + [smem] * 3,
+        in_specs=[vmem] * 16,
         out_specs=[hbm] * 2,
         scratch_shapes=[
             pltpu.VMEM((width, SLOT, depth), F32),
@@ -519,7 +539,7 @@
         ],
         compiler_params=params,
         name="late_x_steps",
-    )(*early, outer, labels, kern_x, bind_table, release_table)
+    )(*early, outer, labels, spread)
     return grad, adjoint
 
 

time: 32.5 us -> 30.7 us (0.945)
  waiting for transfers between devices: 3.92 us -> 10.6 us
  starting transfers between devices: 15.1 us -> 8.87 us
  Pallas kernels: 10.3 us -> 8.02 us
    ppermute x1, waiting for transfers between devices: 0.71 us -> 7.36 us  [shards(): two = lax.ppermute(two, AXES, swap_along_gy(shape, 1))]
    ppermute x1, starting transfers between devices: 8.83 us -> 2.94 us  [shards(): outer = lax.ppermute(outer, AXES, across)]
    ppermute x1, waiting for transfers between devices: 0.01 us -> 2.5 us  [shards(): outer = lax.ppermute(outer, AXES, across)]
    ppermute x1, waiting for transfers between devices: 3.19 us -> 0.75 us  [shards(): one = lax.ppermute(one, AXES, swap_along_gy(shape, 0))]
    pallas_call x4, Pallas kernels: 8.63 us -> 6.28 us  [the longest x1 3.65 us: shards(): pl.pallas_call(functools.partial(last_kernel, reach), out_shape=[array(ti...]
    ppermute x1, starting transfers between devices: 3.48 us -> 3.12 us  [shards(): one = lax.ppermute(one, AXES, swap_along_gy(shape, 0))]
  transfers between devices with their start and end apart: 3 -> 3, of which waited for: 2 -> 3; matrix products, arithmetic and copies ran while one was open for 0% -> 0% of each run, Pallas kernels for 10% -> 7%
where the time goes in v4:
time: 30.7 us; the launch traced here: 30.5 us
  waiting for transfers between devices  10.6 us (35%)
  starting transfers between devices  8.87 us (29%)
  Pallas kernels  8.02 us (26%)
  blocking collectives  2.25 us (7%)
  between operations  0.72 us (2%)
    ppermute x1, waiting for transfers between devices, shards(): two = lax.ppermute(two, AXES, swap_along_gy(shape, 1))  7.36 us
    pallas_call x1, Pallas kernels, shards(): pl.pallas_call(functools.partial(last_kernel, reach), out_shape=[array(ti...  3.65 us
    ppermute x1, starting transfers between devices, shards(): one = lax.ppermute(one, AXES, swap_along_gy(shape, 0))  3.12 us
    ppermute x1, starting transfers between devices, shards(): outer = lax.ppermute(outer, AXES, across)  2.94 us
    ppermute x1, starting transfers between devices, shards(): two = lax.ppermute(two, AXES, swap_along_gy(shape, 1))  2.81 us
    ppermute x1, waiting for transfers between devices, shards(): outer = lax.ppermute(outer, AXES, across)  2.5 us
    all_gather x1, blocking collectives, shards(): inner = lax.all_gather(inner, AXES, axis_index_groups=within)  2.25 us
    pallas_call x1, Pallas kernels, shards(): pl.pallas_call(functools.partial(first_kernel, reach), out_shape=[array((...  1.74 us
  transfers between devices with their start and end apart: 3, of which 3 were waited for; matrix products, arithmetic and copies ran while one was open for 0% of the time, Pallas kernels for 7%

profile of v4, /device:TPU:281, one launch (start us, length us, event | category | flops | bytes accessed | tf_op | source)
XLA Modules:
  0.0 30.5 jit_solution(13239806638208002543)
XLA Ops:
  0.6 0.0 copy-start
  0.6 0.0 copy-start.1
  0.7 0.0 copy-start.2
  0.7 1.7 %weigh_blur_z.1 = (f32[24,24,128]{2,1,0:T(8,128)S(1)}, f32[22,24,128]{2,1,0:T(8,128)S(1)}, f32[22,24,128]{2,1,0:T(8,128)S(1)}, f32[68,8,128]{2,1,0:T(8,128)S(1)}) custom-call(f32[576,128]{1,0:T(8,128)} %bitcast.8, s32[576,128]{1,0:T(8,128)} %bitcast.9, s32[576,128]{1,0:T(8,128)} %bitcast.5, f32[576,128]{1,0:T(8,128)} %bitcast.6, ...), custom_call_target="tpu_custom_call" | custom-call | tf_op jit(solution)/shard_map/weigh_blur_z/pallas_call | solution.py:463
  2.4 3.1 %collective-permute-start = (f32[22,24,128]{2,1,0:T(8,128)S(1)}, f32[22,24,128]{2,1,0:T(8,128)S(1)}, u32[]{:S(2)}, u32[]{:S(2)}) collective-permute-start(f32[22,24,128]{2,1,0:T(8,128)S(1)} %get-tuple-element.24), channel_id=1, source_target_pairs={{1,2},{2,1},{3,4},{4,3},{5,6},{6,5},{7,8},{8,7},{9,10},{10,9},{11,... | collective-permute-start | bytes 811016 | tf_op jit(solution)/shard_map/ppermute | solution.py:477
  5.5 2.8 %collective-permute-start.1 = (f32[22,24,128]{2,1,0:T(8,128)S(1)}, f32[22,24,128]{2,1,0:T(8,128)S(1)}, u32[]{:S(2)}, u32[]{:S(2)}) collective-permute-start(f32[22,24,128]{2,1,0:T(8,128)S(1)} %get-tuple-element.25), channel_id=1, source_target_pairs={{0,1},{1,0},{2,3},{3,2},{4,5},{5,4},{6,7},{7,6},{8,9},{9,8},{10,11... | collective-permute-start | bytes 811016 | tf_op jit(solution)/shard_map/ppermute | solution.py:478
  8.4 0.5 %own_y.1.part = f32[28,24,128]{2,1,0:T(8,128)S(1)} custom-call(f32[24,24,128]{2,1,0:T(8,128)S(1)} %get-tuple-element.22.own, f32[68,8,128]{2,1,0:T(8,128)S(1)} %get-tuple-element.23.spread), custom_call_target="tpu_custom_call" | custom-call | flops 4000000 | bytes 700000 | tf_op jit(solution)/shard_map/own_y/pallas_call | solution.py:480
  8.9 0.8 %collective-permute-done.one = f32[22,24,128]{2,1,0:T(8,128)S(1)} collective-permute-done((f32[22,24,128]{2,1,0:T(8,128)S(1)}, f32[22,24,128]{2,1,0:T(8,128)S(1)}, u32[]{:S(2)}, u32[]{:S(2)}) %collective-permute-start) | collective-permute-done | bytes 270368 | tf_op jit(solution)/shard_map/ppermute | solution.py:477
  9.6 7.4 %collective-permute-done.1.two = f32[22,24,128]{2,1,0:T(8,128)S(1)} collective-permute-done((f32[22,24,128]{2,1,0:T(8,128)S(1)}, f32[22,24,128]{2,1,0:T(8,128)S(1)}, u32[]{:S(2)}, u32[]{:S(2)}) %collective-permute-start.1) | collective-permute-done | bytes 270368 | tf_op jit(solution)/shard_map/ppermute | solution.py:478
  17.0 0.0 copy-done
  17.0 0.0 copy-done.1
  17.0 0.0 copy-done.2
  17.0 0.4 %rest_y.1 = (f32[768,128]{1,0:T(8,128)S(1)}, f32[604,128]{1,0:T(8,128)S(1)}, f32[604,128]{1,0:T(8,128)S(1)}) custom-call(f32[28,24,128]{2,1,0:T(8,128)S(1)} %own_y.1.part, f32[22,24,128]{2,1,0:T(8,128)S(1)} %collective-permute-done.one, f32[22,24,128]{2,1,0:T(8,128)S(1)} %collective-permute-done.1.two, s32[24,24,128]{2,1,0:T(8,128)S(1)} %copy-done, ...), custom_call_target="tpu_custom_call" | custom-call | tf_op jit(solution)/shard_map/rest_y/pallas_call | solution.py:492
  17.4 2.9 %collective-permute-start.2 = (f32[604,128]{1,0:T(8,128)S(1)}, f32[604,128]{1,0:T(8,128)S(1)}, u32[]{:S(2)}, u32[]{:S(2)}) collective-permute-start(f32[604,128]{1,0:T(8,128)S(1)} %get-tuple-element.41), channel_id=1, source_target_pairs={{32,64},{64,32},{33,65},{65,33},{34,66},{66,34},{35,67},{67,35},{3... | collective-permute-start | bytes 927752 | tf_op jit(solution)/shard_map/ppermute | solution.py:509
  20.3 2.3 %all-gather.1.inner = f32[2,604,128]{2,1,0:T(8,128)S(1)} all-gather(f32[1,604,128]{2,1,0:T(8,128)S(1)} %bitcast.7), channel_id=2, replica_groups={{0,32},{1,33},{2,34},{3,35},{4,36},{5,37},{6,38},{7,39},{8,40},{9,41},{..., dimensions={0}, use_global_device_ids=true | all-gather | bytes 927744 | tf_op jit(solution)/shard_map/all_gather | solution.py:510
  22.6 1.7 %early_x.1 = (f32[28,40,128]{2,1,0:T(8,128)S(1)}, f32[28,40,128]{2,1,0:T(8,128)S(1)}, f32[2,28,40,128]{3,2,1,0:T(8,128)S(1)}, f32[28,40,128]{2,1,0:T(8,128)S(1)}...) custom-call(f32[768,128]{1,0:T(8,128)S(1)} %get-tuple-element.26.blu, ...), custom_call_target="tpu_custom_call" | custom-call | flops 8000000 | bytes 3000000 | tf_op jit(solution)/shard_map/early_x/pallas_call | solution.py:514
  24.3 2.5 %collective-permute-done.2.outer = f32[604,128]{1,0:T(8,128)S(1)} collective-permute-done((f32[604,128]{1,0:T(8,128)S(1)}, f32[604,128]{1,0:T(8,128)S(1)}, u32[]{:S(2)}, u32[]{:S(2)}) %collective-permute-start.2) | collective-permute-done | bytes 309280 | tf_op jit(solution)/shard_map/ppermute | solution.py:509
  26.8 3.7 %late_x_steps.1 = (f32[24,24,128]{2,1,0:T(8,128)}, f32[2,24,24,128]{3,2,1,0:T(8,128)}) custom-call(f32[28,40,128]{2,1,0:T(8,128)S(1)} %get-tuple-element.28.part, f32[28,40,128]{2,1,0:T(8,128)S(1)} %get-tuple-element.29.coef, f32[2,28,40,128]{3,2,1,0:T(8,128)S(1)} %get-tuple-element.30.state, f32[28,40,128]{2,1,0:T(8,128)S(1)} %get-tuple-element.31.keep, ...), custom_call_target="tpu_custom_call" | custom-call | tf_op jit(solution)/shard_map/late_x_steps/pallas_call | solution.py:526
Async XLA Ops:
  0.6 16.3 %copy-start = (s32[24,24,128]{2,1,0:T(8,128)S(1)}, s32[24,24,128]{2,1,0:T(8,128)}, u32[]{:S(2)}) copy-start(s32[24,24,128]{2,1,0:T(8,128)} %labels.5) | copy-start | bytes 884740
  0.6 16.3 %copy-start.1 = (f32[24,24,128]{2,1,0:T(8,128)S(1)}, f32[24,24,128]{2,1,0:T(8,128)}, u32[]{:S(2)}) copy-start(f32[24,24,128]{2,1,0:T(8,128)} %diffusion.3) | copy-start | bytes 884740
  0.7 16.3 %copy-start.2 = (bf16[2,24,24,128]{3,2,1,0:T(8,128)(2,1)S(1)}, bf16[2,24,24,128]{3,2,1,0:T(8,128)(2,1)}, u32[]{:S(2)}) copy-start(bf16[2,24,24,128]{3,2,1,0:T(8,128)(2,1)} %states.3) | copy-start | bytes 884740
  2.4 7.2 %collective-permute-start = (f32[22,24,128]{2,1,0:T(8,128)S(1)}, f32[22,24,128]{2,1,0:T(8,128)S(1)}, u32[]{:S(2)}, u32[]{:S(2)}) collective-permute-start(f32[22,24,128]{2,1,0:T(8,128)S(1)} %get-tuple-element.24), channel_id=1, source_target_pairs={{1,2},{2,1},{3,4},{4,3},{5,6},{6,5},{7,8},{8,7},{9,10},{10,9},{11,... | collective-permute-start | bytes 811016 | tf_op jit(solution)/shard_map/ppermute | solution.py:477
  5.5 11.4 %collective-permute-start.1 = (f32[22,24,128]{2,1,0:T(8,128)S(1)}, f32[22,24,128]{2,1,0:T(8,128)S(1)}, u32[]{:S(2)}, u32[]{:S(2)}) collective-permute-start(f32[22,24,128]{2,1,0:T(8,128)S(1)} %get-tuple-element.25), channel_id=1, source_target_pairs={{0,1},{1,0},{2,3},{3,2},{4,5},{5,4},{6,7},{7,6},{8,9},{9,8},{10,11... | collective-permute-start | bytes 811016 | tf_op jit(solution)/shard_map/ppermute | solution.py:478
  17.4 9.4 %collective-permute-start.2 = (f32[604,128]{1,0:T(8,128)S(1)}, f32[604,128]{1,0:T(8,128)S(1)}, u32[]{:S(2)}, u32[]{:S(2)}) collective-permute-start(f32[604,128]{1,0:T(8,128)S(1)} %get-tuple-element.41), channel_id=1, source_target_pairs={{32,64},{64,32},{33,65},{65,33},{34,66},{66,34},{35,67},{67,35},{3... | collective-permute-start | bytes 927752 | tf_op jit(solution)/shard_map/ppermute | solution.py:509

commit v5 on v4

--- a/solution.py
+++ b/solution.py
@@ -14,6 +14,7 @@
 HIGH = 40
 CHUNKS = 4
 F32 = jnp.float32
+STEP_ROWS = tuple(slice(JOFF - RIM + k, JOFF - RIM + k + SLOT) for k in (0, -1, 1))
 
 
 def blur(read, write, taps, outs, sources, group=14, base=None):
@@ -54,7 +55,7 @@
 
 def first_kernel(reach, misfit_h, mask_h, labels_h, diffusion_h, states_h, kern_h, *rest):
     few_h, rest = rest[:4], rest[4:]
-    own, one, two, spread, misfit, mask, labels, diffusion, states, kern, work, edge, *few, sems = rest
+    own, one, two, spread, labels, diffusion, states, misfit, mask, kern, work, edge, *few, sems = rest
     steps, nx, ny, depth = states.shape
     copies = [pltpu.make_async_copy(a, b, sems.at[n]) for n, (a, b) in enumerate(
         ((kern_h, kern), (misfit_h, misfit), (mask_h, mask), (diffusion_h, diffusion), (labels_h, labels), (states_h, states), *zip(few_h, few)))]
@@ -195,13 +196,68 @@
     return lax.broadcasted_iota(jnp.int32, (rows, depth), 1) < depth - 1
 
 
+def stepper(image, adj, coef, state, keep, cx, cy, cz, xl, xu, yl, yu, zl, zu, labels, bind_t, release_t, put):
+    steps, ny, depth = state.shape[0], labels.shape[1], labels.shape[2]
+    h, down, after = STEP_ROWS
+    own_rows = slice(JOFF, JOFF + ny)
+    before, next_ = slice(JOFF - 1, JOFF - 1 + ny), slice(JOFF + 1, JOFF + 1 + ny)
+
+    def first(p, c_low, c_up, c_y, c_y_low, c_z, kept):
+        a = image[p, h, :]
+        total = c_up * (image[p + 1, h, :] - a) + c_low * (image[p - 1, h, :] - a)
+        total += c_y * (image[p, after, :] - a) + c_y_low * (image[p, down, :] - a)
+        fz = c_z * (pltpu.roll(a, depth - 1, 1) - a)
+        adj[p, h, :] = kept * a + total + (fz - pltpu.roll(fz, 1, 1))
+
+    def first_plain(p):
+        first(p, cx[p - 1, h, :], cx[p, h, :], cy[p, h, :], cy[p, down, :], cz[p, h, :], keep[p, h, :])
+
+    def second(p, c_low, s_low, state_low, c_up, s_up, state_up):
+        at = own_rows
+        a1, a0 = image[p, at, :], adj[p, at, :]
+        s1, s0 = state[steps - 1, p, at, :], state[0, p, at, :]
+        total, slopes = 0.0, 0.0
+
+        def face(c, s, i, rows, states):
+            change1, change0 = image[i, rows, :] - a1, adj[i, rows, :] - a0
+            return c * change0, s * ((states[0] - s1) * change1 + (states[1] - s0) * change0)
+
+        x = p - RIM
+        for f, g in (face(c_low, s_low, p - 1, at, state_low), face(c_up, s_up, p + 1, at, state_up),
+                     face(cy[p, before, :], yu[p, before, :], p, before,
+                          (state[steps - 1, p, before, :], state[0, p, before, :])),
+                     face(cy[p, at, :], yl[p, at, :], p, next_, (state[steps - 1, p, next_, :], state[0, p, next_, :]))):
+            total, slopes = total + f, slopes + g
+        nxt = functools.partial(pltpu.roll, shift=depth - 1, axis=1)
+        change1, change0 = nxt(a1) - a1, nxt(a0) - a0
+        both = (nxt(s1) - s1) * change1 + (nxt(s0) - s0) * change0
+        fz = cz[p, at, :] * change0
+        total += fz - pltpu.roll(fz, 1, 1)
+        slopes += zl[p, at, :] * both + pltpu.roll(zu[p, at, :] * both, 1, 1)
+        code = labels[x]
+        bind, release = rate(code, bind_t), rate(code, release_t)
+        b1 = 0.5 * a1 + release * (a1 - 0.5 * a1)
+        put(x, -slopes, a0 + total + bind * (b1 - a0), b1 + release * (a0 - b1))
+
+    def second_plain(p):
+        at = own_rows
+        second(p, cx[p - 1, at, :], xu[p - 1, at, :], (state[steps - 1, p - 1, at, :], state[0, p - 1, at, :]),
+               cx[p, at, :], xl[p, at, :], (state[steps - 1, p + 1, at, :], state[0, p + 1, at, :]))
+
+    return first, first_plain, second, second_plain
+
+
+def free_slots(nx, width, even):
+    return jnp.where(even, width + RIM, RIM), nx - width
+
+
 def early_x_kernel(reach, blurred, inner, one, two, labels, diffusion, states, spread,
-                   image, coef, state, keep, cx, cy, cz, xl, xu, yl, yu, zl, zu, ext, kind):
+                   image, coef, state, keep, cx, cy, cz, xl, xu, yl, yu, zl, zu, done_adj, done, ext, kind, adj):
     nx, ny, depth = labels.shape
     steps = states.shape[0]
-    taps_at, _, bind_at, _ = vectors(spread, reach)
+    taps_at, _, bind_at, release_at = vectors(spread, reach)
     taps = [spread[t] for t in taps_at]
-    bind_t = [spread[t, 0:1, :] for t in bind_at]
+    bind_t, release_t = ([spread[t, 0:1, :] for t in at] for at in (bind_at, release_at))
     width = (len(taps) - 1) // 2 + RIM
     tall = ny + 2 * RIM
     lo, own_rows = JOFF - RIM, slice(JOFF, JOFF + ny)
@@ -283,9 +339,32 @@
             up[p, h, :] = 2.0 * r * r
         keep[p, h, :] = 1.0 - 0.5 * rate(kind[p, h, :], bind_t)
 
+    even = is_even()
+    lower, count = free_slots(nx, width, even)
+
+    def put(x, *results):
+        for n, value in enumerate(results):
+            done[n, x + RIM - lower] = value
+
+    _, first, _, second = stepper(image, adj, coef, state, keep, cx, cy, cz, xl, xu, yl, yu, zl, zu, labels, bind_t, release_t, put)
+
+    @pl.loop(0, count + 2, unroll=count + 2)
+    def _(n):
+        first(lower - 1 + n)
+
+    @pl.loop(0, count, unroll=count)
+    def _(n):
+        second(lower + n)
+
+    def keep_nearest(even):
+        for n in range(2):
+            done_adj[n] = adj[width + 1 + n if even else nx + 2 * RIM - 2 - width - n]
+
+    both_ways(even, keep_nearest)
+
 
 def last_kernel(reach, part, coef, state, keep, cx, cy, cz, xl, xu, yl, yu, zl, zu, outer, labels, spread,
-                grad_h, adjoint_h, ext, image, adj, rim, grad, adjoint, sems):
+                done_adj, done, grad_h, adjoint_h, ext, image, adj, rim, grad, adjoint, sems):
     nx, ny, depth = labels.shape
     steps = state.shape[0]
     taps_at, _, bind_at, release_at = vectors(spread, reach)
@@ -297,6 +376,13 @@
     outs = range(nx + 2 * RIM)
     even = is_even()
 
+    lower, count = free_slots(nx, width, even)
+    at = pl.ds(lower - RIM, count)
+    copies = [pltpu.make_async_copy(done.at[n], target, sems.at[CHUNKS + 1, n])
+              for n, target in enumerate((grad_h.at[at], adjoint_h.at[0, at], adjoint_h.at[1, at]))]
+    for c in copies:
+        c.start()
+
     for k in range(width):
         ext[k, lo:lo + tall, :] = outer[pl.ds(k * tall, tall), :]
     for k in range(RIM):
@@ -324,51 +410,16 @@
 
         both_ways(even, add)
 
-    h = slice(JOFF - RIM, JOFF - RIM + SLOT)
-    down = slice(h.start - 1, h.stop - 1)
-    after = slice(h.start + 1, h.stop + 1)
-
-    def first(p, c_low, c_up, c_y, c_y_low, c_z, kept):
-        a = image[p, h, :]
-        total = c_up * (image[p + 1, h, :] - a) + c_low * (image[p - 1, h, :] - a)
-        total += c_y * (image[p, after, :] - a) + c_y_low * (image[p, down, :] - a)
-        fz = c_z * (pltpu.roll(a, depth - 1, 1) - a)
-        adj[p, h, :] = kept * a + total + (fz - pltpu.roll(fz, 1, 1))
+    def put(x, *results):
+        grad[x], adjoint[0, x], adjoint[1, x] = results
+
+    first, first_plain, second, second_plain = stepper(
+        image, adj, coef, state, keep, cx, cy, cz, xl, xu, yl, yu, zl, zu, labels, bind_t, release_t, put)
+    h, down, after = STEP_ROWS
 
     def coupling(here, there):
         q, _ = shares(here, there)
         return 2.0 * here * q
-
-    before, next_ = slice(JOFF - 1, JOFF - 1 + ny), slice(JOFF + 1, JOFF + 1 + ny)
-
-    def second(p, c_low, s_low, state_low, c_up, s_up, state_up):
-        at = own_rows
-        a1, a0 = image[p, at, :], adj[p, at, :]
-        s1, s0 = state[steps - 1, p, at, :], state[0, p, at, :]
-        total, slopes = 0.0, 0.0
-
-        def face(c, s, i, rows, states):
-            change1, change0 = image[i, rows, :] - a1, adj[i, rows, :] - a0
-            return c * change0, s * ((states[0] - s1) * change1 + (states[1] - s0) * change0)
-
-        x = p - RIM
-        for f, g in (face(c_low, s_low, p - 1, at, state_low), face(c_up, s_up, p + 1, at, state_up),
-                     face(cy[p, before, :], yu[p, before, :], p, before,
-                          (state[steps - 1, p, before, :], state[0, p, before, :])),
-                     face(cy[p, at, :], yl[p, at, :], p, next_, (state[steps - 1, p, next_, :], state[0, p, next_, :]))):
-            total, slopes = total + f, slopes + g
-        nxt = functools.partial(pltpu.roll, shift=depth - 1, axis=1)
-        change1, change0 = nxt(a1) - a1, nxt(a0) - a0
-        both = (nxt(s1) - s1) * change1 + (nxt(s0) - s0) * change0
-        fz = cz[p, at, :] * change0
-        total += fz - pltpu.roll(fz, 1, 1)
-        slopes += zl[p, at, :] * both + pltpu.roll(zu[p, at, :] * both, 1, 1)
-        code = labels[x]
-        bind, release = rate(code, bind_t), rate(code, release_t)
-        b1 = 0.5 * a1 + release * (a1 - 0.5 * a1)
-        grad[x] = -slopes
-        adjoint[0, x] = a0 + total + bind * (b1 - a0)
-        adjoint[1, x] = b1 + release * (a0 - b1)
 
     def send(n, x, count):
         at = pl.ds(x, count)
@@ -402,31 +453,35 @@
 
     both_ways(even, near_rim)
 
-    @pl.loop(0, nx, unroll=8)
+    def take(even):
+        for n in range(2):
+            adj[width + 1 + n if even else nx + 2 * RIM - 2 - width - n] = done_adj[n]
+
+    both_ways(even, take)
+    left = width - RIM
+    low = jnp.where(even, RIM + 1, nx + 1 - left)
+
+    @pl.loop(0, left, unroll=5)
     def _(n):
-        p = n + jnp.where(even, RIM + 1, 1)
-        first(p, cx[p - 1, h, :], cx[p, h, :], cy[p, h, :], cy[p, down, :], cz[p, h, :], keep[p, h, :])
+        first_plain(low + n)
 
     both_ways(even, near_rim_second)
-    copies = send(0, jnp.where(even, 0, nx - 1), 1)
-    for c in copies:
+    more = send(0, jnp.where(even, 0, nx - 1), 1)
+    for c in more:
         c.start()
-    base = jnp.where(even, RIM + 1, RIM)
-    size = -(-(nx - 1) // CHUNKS)
+    copies += more
+    base = jnp.where(even, RIM + 1, nx - left)
+    size = (left + 1) // CHUNKS
+
+    @pl.loop(0, CHUNKS)
+    def _(n):
+        for k in range(size):
+            second_plain(base + n * size + k)
+        for c in send(n + 1, base - RIM + n * size, size):
+            c.start()
+
     for n in range(CHUNKS):
-        count = min(size, nx - 1 - n * size)
-
-        @pl.loop(n * size, n * size + count, unroll=count)
-        def _(k):
-            p = base + k
-            at = own_rows
-            second(p, cx[p - 1, at, :], xu[p - 1, at, :], (state[steps - 1, p - 1, at, :], state[0, p - 1, at, :]),
-                   cx[p, at, :], xl[p, at, :], (state[steps - 1, p + 1, at, :], state[0, p + 1, at, :]))
-
-        more = send(n + 1, base - RIM + n * size, count)
-        for c in more:
-            c.start()
-        copies += more
+        copies += send(n + 1, base - RIM + n * size, size)
     for c in copies:
         c.wait()
 
@@ -460,20 +515,21 @@
     slots = width + RIM + 1 + steps
     slab = array((slots, nx, depth), F32)
     few = (kern_x, kern_y, bind_table, release_table)
-    own, one, two, spread = pl.pallas_call(
+    own, one, two, spread, held_labels, held_diffusion, held_states = pl.pallas_call(
         functools.partial(first_kernel, reach),
-        out_shape=[array((ny, nx, depth), F32), slab, slab, array((sum(t.shape[0] for t in few), 8, depth), F32)],
+        out_shape=[array((ny, nx, depth), F32), slab, slab, array((sum(t.shape[0] for t in few), 8, depth), F32),
+                   array(flat, jnp.int32), array(flat, F32), array(free_states.shape, free_states.dtype)],
         in_specs=[hbm] * (6 + len(few)),
-        out_specs=[vmem] * 4,
+        out_specs=[vmem] * 7,
         scratch_shapes=[
-            pltpu.VMEM(flat, F32), pltpu.VMEM(flat, jnp.int32), pltpu.VMEM(flat, jnp.int32), pltpu.VMEM(flat, F32),
-            pltpu.VMEM(free_states.shape, free_states.dtype), pltpu.SMEM(kern_z.shape, F32),
+            pltpu.VMEM(flat, F32), pltpu.VMEM(flat, jnp.int32), pltpu.SMEM(kern_z.shape, F32),
             pltpu.VMEM(flat, F32), pltpu.VMEM((steps * nx * ny, depth), F32),
             *(pltpu.SMEM(t.shape, F32) for t in few), pltpu.SemaphoreType.DMA((6 + len(few),))],
         compiler_params=params,
         name="weigh_blur_z",
     )(in_hbm(misfit.reshape(flat)), in_hbm(bleach_mask.reshape(flat)), in_hbm(labels.reshape(flat)),
       in_hbm(diffusion.reshape(flat)), in_hbm(free_states), in_hbm(kern_z), *map(in_hbm, few))
+    labels, diffusion = held_labels.reshape(labels.shape), held_diffusion.reshape(diffusion.shape)
     one = lax.ppermute(one, AXES, swap_along_gy(shape, 0))
     two = lax.ppermute(two, AXES, swap_along_gy(shape, 1))
 
@@ -497,7 +553,7 @@
         scratch_shapes=[pltpu.VMEM((slots, nx, depth), F32)] * 2,
         compiler_params=params,
         name="rest_y",
-    )(part, one, two, labels, diffusion, free_states, spread)
+    )(part, one, two, labels, diffusion, held_states, spread)
 
     line = shape[1]
     across = []
@@ -511,22 +567,23 @@
 
     around = (nx + 2 * RIM, HIGH, depth)
     field = array(around, F32)
-    early = pl.pallas_call(
+    *early, done_adj, done = pl.pallas_call(
         functools.partial(early_x_kernel, reach),
-        out_shape=[field, field, array((steps, *around), F32)] + [field] * 10,
+        out_shape=[field, field, array((steps, *around), F32)] + [field] * 10
+        + [array((2, *around[1:]), F32), array((3, nx - width, ny, depth), F32)],
         in_specs=[vmem] * 8,
-        out_specs=[vmem] * 13,
-        scratch_shapes=[pltpu.VMEM((width, SLOT, depth), F32), pltpu.VMEM(around, F32)],
+        out_specs=[vmem] * 15,
+        scratch_shapes=[pltpu.VMEM((width, SLOT, depth), F32), pltpu.VMEM(around, F32), pltpu.VMEM(around, F32)],
         compiler_params=params,
         cost_estimate=pl.CostEstimate(flops=8_000_000, bytes_accessed=3_000_000, transcendentals=0),
         name="early_x",
-    )(blurred, inner, one, two, labels, diffusion, free_states, spread)
+    )(blurred, inner, one, two, labels, diffusion, held_states, spread)
 
     tile = (nx, ny, depth)
     grad, adjoint = pl.pallas_call(
         functools.partial(last_kernel, reach),
         out_shape=[array(tile, F32), array((2, *tile), F32)],
-        in_specs=[vmem] * 16,
+        in_specs=[vmem] * 18,
         out_specs=[hbm] * 2,
         scratch_shapes=[
             pltpu.VMEM((width, SLOT, depth), F32),
@@ -535,11 +592,11 @@
             pltpu.VMEM((RIM + 1 + steps, HIGH, depth), F32),
             pltpu.VMEM(tile, F32),
             pltpu.VMEM((2, *tile), F32),
-            pltpu.SemaphoreType.DMA((CHUNKS + 1, 3)),
+            pltpu.SemaphoreType.DMA((CHUNKS + 2, 3)),
         ],
         compiler_params=params,
         name="late_x_steps",
-    )(*early, outer, labels, spread)
+    )(*early, outer, labels, spread, done_adj, done)
     return grad, adjoint
 
 

time: 30.7 us -> 29.8 us (0.971)
  waiting for transfers between devices: 10.6 us -> 10 us
    pallas_call x1, Pallas kernels: 3.65 us -> 2.94 us  [shards(): pl.pallas_call(functools.partial(last_kernel, reach), out_shape=[array(ti...]
    pallas_call x1, Pallas kernels: 1.72 us -> 2.29 us  [shards(): pl.pallas_call(functools.partial(early_x_kernel, reach), out_shape=[field...]
    ppermute x1, waiting for transfers between devices: 2.5 us -> 1.94 us  [shards(): outer = lax.ppermute(outer, AXES, across)]
  transfers between devices with their start and end apart: 3 -> 3, of which waited for: 3 -> 3; matrix products, arithmetic and copies ran while one was open for 0% -> 0% of each run, Pallas kernels for 7% -> 9%
where the time goes in v5:
time: 29.8 us; the launch traced here: 29.7 us
  waiting for transfers between devices  10 us (34%)
  starting transfers between devices  8.87 us (30%)
  Pallas kernels  7.8 us (26%)
  blocking collectives  2.25 us (8%)
  between operations  0.69 us (2%)
    ppermute x1, waiting for transfers between devices, shards(): two = lax.ppermute(two, AXES, swap_along_gy(shape, 1))  7.35 us
    ppermute x1, starting transfers between devices, shards(): one = lax.ppermute(one, AXES, swap_along_gy(shape, 0))  3.12 us
    pallas_call x1, Pallas kernels, shards(): pl.pallas_call(functools.partial(last_kernel, reach), out_shape=[array(ti...  2.94 us
    ppermute x1, starting transfers between devices, shards(): outer = lax.ppermute(outer, AXES, across)  2.93 us
    ppermute x1, starting transfers between devices, shards(): two = lax.ppermute(two, AXES, swap_along_gy(shape, 1))  2.81 us
    pallas_call x1, Pallas kernels, shards(): pl.pallas_call(functools.partial(early_x_kernel, reach), out_shape=[field...  2.29 us
    all_gather x1, blocking collectives, shards(): inner = lax.all_gather(inner, AXES, axis_index_groups=within)  2.25 us
    ppermute x1, waiting for transfers between devices, shards(): outer = lax.ppermute(outer, AXES, across)  1.94 us
  transfers between devices with their start and end apart: 3, of which 3 were waited for; matrix products, arithmetic and copies ran while one was open for 0% of the time, Pallas kernels for 9%

profile of v5, /device:TPU:281, one launch (start us, length us, event | category | flops | bytes accessed | tf_op | source)
XLA Modules:
  0.0 29.7 jit_solution(4036482867075648502)
XLA Ops:
  0.6 1.7 %weigh_blur_z.1 = (f32[24,24,128]{2,1,0:T(8,128)S(1)}, f32[22,24,128]{2,1,0:T(8,128)S(1)}, f32[22,24,128]{2,1,0:T(8,128)S(1)}, f32[68,8,128]{2,1,0:T(8,128)S(1)}...) custom-call(f32[576,128]{1,0:T(8,128)} %bitcast.13, s32[576,128]{1,0:T(8,128)} %bitcast.14, ...), custom_call_target="tpu_custom_call" | custom-call | tf_op jit(solution)/shard_map/weigh_blur_z/pallas_call | solution.py:518
  2.3 3.1 %collective-permute-start = (f32[22,24,128]{2,1,0:T(8,128)S(1)}, f32[22,24,128]{2,1,0:T(8,128)S(1)}, u32[]{:S(2)}, u32[]{:S(2)}) collective-permute-start(f32[22,24,128]{2,1,0:T(8,128)S(1)} %get-tuple-element.29), channel_id=1, source_target_pairs={{1,2},{2,1},{3,4},{4,3},{5,6},{6,5},{7,8},{8,7},{9,10},{10,9},{11,... | collective-permute-start | bytes 811016 | tf_op jit(solution)/shard_map/ppermute | solution.py:533
  5.4 2.8 %collective-permute-start.1 = (f32[22,24,128]{2,1,0:T(8,128)S(1)}, f32[22,24,128]{2,1,0:T(8,128)S(1)}, u32[]{:S(2)}, u32[]{:S(2)}) collective-permute-start(f32[22,24,128]{2,1,0:T(8,128)S(1)} %get-tuple-element.30), channel_id=1, source_target_pairs={{0,1},{1,0},{2,3},{3,2},{4,5},{5,4},{6,7},{7,6},{8,9},{9,8},{10,11... | collective-permute-start | bytes 811016 | tf_op jit(solution)/shard_map/ppermute | solution.py:534
  8.3 0.5 %own_y.1.part = f32[28,24,128]{2,1,0:T(8,128)S(1)} custom-call(f32[24,24,128]{2,1,0:T(8,128)S(1)} %get-tuple-element.27.own, f32[68,8,128]{2,1,0:T(8,128)S(1)} %get-tuple-element.28.spread), custom_call_target="tpu_custom_call" | custom-call | flops 4000000 | bytes 700000 | tf_op jit(solution)/shard_map/own_y/pallas_call | solution.py:536
  8.8 0.8 %collective-permute-done.one = f32[22,24,128]{2,1,0:T(8,128)S(1)} collective-permute-done((f32[22,24,128]{2,1,0:T(8,128)S(1)}, f32[22,24,128]{2,1,0:T(8,128)S(1)}, u32[]{:S(2)}, u32[]{:S(2)}) %collective-permute-start) | collective-permute-done | bytes 270368 | tf_op jit(solution)/shard_map/ppermute | solution.py:533
  9.5 7.4 %collective-permute-done.1.two = f32[22,24,128]{2,1,0:T(8,128)S(1)} collective-permute-done((f32[22,24,128]{2,1,0:T(8,128)S(1)}, f32[22,24,128]{2,1,0:T(8,128)S(1)}, u32[]{:S(2)}, u32[]{:S(2)}) %collective-permute-start.1) | collective-permute-done | bytes 270368 | tf_op jit(solution)/shard_map/ppermute | solution.py:534
  16.9 0.4 %rest_y.1 = (f32[768,128]{1,0:T(8,128)S(1)}, f32[604,128]{1,0:T(8,128)S(1)}, f32[604,128]{1,0:T(8,128)S(1)}) custom-call(f32[28,24,128]{2,1,0:T(8,128)S(1)} %own_y.1.part, f32[22,24,128]{2,1,0:T(8,128)S(1)} %collective-permute-done.one, f32[22,24,128]{2,1,0:T(8,128)S(1)} %collective-permute-done.1.two, s32[24,24,128]{2,1,0:T(8,128)S(1)} %bitcast.7, ...), custom_call_target="tpu_custom_call" | custom-call | tf_op jit(solution)/shard_map/rest_y/pallas_call | solution.py:548
  17.3 2.9 %collective-permute-start.2 = (f32[604,128]{1,0:T(8,128)S(1)}, f32[604,128]{1,0:T(8,128)S(1)}, u32[]{:S(2)}, u32[]{:S(2)}) collective-permute-start(f32[604,128]{1,0:T(8,128)S(1)} %get-tuple-element.49), channel_id=1, source_target_pairs={{32,64},{64,32},{33,65},{65,33},{34,66},{66,34},{35,67},{67,35},{3... | collective-permute-start | bytes 927752 | tf_op jit(solution)/shard_map/ppermute | solution.py:565
  20.2 2.3 %all-gather.1.inner = f32[2,604,128]{2,1,0:T(8,128)S(1)} all-gather(f32[1,604,128]{2,1,0:T(8,128)S(1)} %bitcast.12), channel_id=2, replica_groups={{0,32},{1,33},{2,34},{3,35},{4,36},{5,37},{6,38},{7,39},{8,40},{9,41},{..., dimensions={0}, use_global_device_ids=true | all-gather | bytes 927744 | tf_op jit(solution)/shard_map/all_gather | solution.py:566
  22.5 2.3 %early_x.1 = (f32[28,40,128]{2,1,0:T(8,128)S(1)}, f32[28,40,128]{2,1,0:T(8,128)S(1)}, f32[2,28,40,128]{3,2,1,0:T(8,128)S(1)}, f32[28,40,128]{2,1,0:T(8,128)S(1)}...) custom-call(f32[768,128]{1,0:T(8,128)S(1)} %get-tuple-element.34.blu, ...), custom_call_target="tpu_custom_call" | custom-call | flops 8000000 | bytes 3000000 | tf_op jit(solution)/shard_map/early_x/pallas_call | solution.py:570
  24.8 1.9 %collective-permute-done.2.outer = f32[604,128]{1,0:T(8,128)S(1)} collective-permute-done((f32[604,128]{1,0:T(8,128)S(1)}, f32[604,128]{1,0:T(8,128)S(1)}, u32[]{:S(2)}, u32[]{:S(2)}) %collective-permute-start.2) | collective-permute-done | bytes 309280 | tf_op jit(solution)/shard_map/ppermute | solution.py:565
  26.7 2.9 %late_x_steps.1 = (f32[24,24,128]{2,1,0:T(8,128)}, f32[2,24,24,128]{3,2,1,0:T(8,128)}) custom-call(f32[28,40,128]{2,1,0:T(8,128)S(1)} %get-tuple-element.36.part, f32[28,40,128]{2,1,0:T(8,128)S(1)} %get-tuple-element.37.coef, f32[2,28,40,128]{3,2,1,0:T(8,128)S(1)} %get-tuple-element.38.state, f32[28,40,128]{2,1,0:T(8,128)S(1)} %get-tuple-element.39.keep, ...), custom_call_target="tpu_custom_call" | custom-call | tf_op jit(solution)/shard_map/late_x_steps/pallas_call | solution.py:583
Async XLA Ops:
  2.3 7.2 %collective-permute-start = (f32[22,24,128]{2,1,0:T(8,128)S(1)}, f32[22,24,128]{2,1,0:T(8,128)S(1)}, u32[]{:S(2)}, u32[]{:S(2)}) collective-permute-start(f32[22,24,128]{2,1,0:T(8,128)S(1)} %get-tuple-element.29), channel_id=1, source_target_pairs={{1,2},{2,1},{3,4},{4,3},{5,6},{6,5},{7,8},{8,7},{9,10},{10,9},{11,... | collective-permute-start | bytes 811016 | tf_op jit(solution)/shard_map/ppermute | solution.py:533
  5.4 11.4 %collective-permute-start.1 = (f32[22,24,128]{2,1,0:T(8,128)S(1)}, f32[22,24,128]{2,1,0:T(8,128)S(1)}, u32[]{:S(2)}, u32[]{:S(2)}) collective-permute-start(f32[22,24,128]{2,1,0:T(8,128)S(1)} %get-tuple-element.30), channel_id=1, source_target_pairs={{0,1},{1,0},{2,3},{3,2},{4,5},{5,4},{6,7},{7,6},{8,9},{9,8},{10,11... | collective-permute-start | bytes 811016 | tf_op jit(solution)/shard_map/ppermute | solution.py:534
  17.3 9.4 %collective-permute-start.2 = (f32[604,128]{1,0:T(8,128)S(1)}, f32[604,128]{1,0:T(8,128)S(1)}, u32[]{:S(2)}, u32[]{:S(2)}) collective-permute-start(f32[604,128]{1,0:T(8,128)S(1)} %get-tuple-element.49), channel_id=1, source_target_pairs={{32,64},{64,32},{33,65},{65,33},{34,66},{66,34},{35,67},{67,35},{3... | collective-permute-start | bytes 927752 | tf_op jit(solution)/shard_map/ppermute | solution.py:565

commit v6 on v5

--- a/solution.py
+++ b/solution.py
@@ -12,7 +12,7 @@
 JOFF = 4
 SLOT = 32
 HIGH = 40
-CHUNKS = 4
+CHUNKS = 2
 F32 = jnp.float32
 STEP_ROWS = tuple(slice(JOFF - RIM + k, JOFF - RIM + k + SLOT) for k in (0, -1, 1))
 
@@ -41,7 +41,7 @@
 
 
 def right_comes_first():
-    return (lax.axis_index("gx") + lax.axis_index("gy")) % 2 == 1
+    return (lax.axis_index("gx") + lax.axis_index("gx") // 2 + lax.axis_index("gy")) % 2 == 1
 
 
 def is_even():
@@ -405,7 +405,7 @@
             blur(lambda e: ext[width - 1 - e if even else e - width - nx, rows, :], write, taps, touched, far,
                  base=lambda i: part[i, rows, :])
             for i in outs:
-                if i not in touched:
+                if i not in touched and min(abs(i - k) for k in touched) <= 3:
                     image[i, rows, :] = part[i, rows, :]
 
         both_ways(even, add)
@@ -461,7 +461,7 @@
     left = width - RIM
     low = jnp.where(even, RIM + 1, nx + 1 - left)
 
-    @pl.loop(0, left, unroll=5)
+    @pl.loop(0, left, unroll=left)
     def _(n):
         first_plain(low + n)
 
@@ -490,7 +490,7 @@
     nx, ny = shape
     pairs = []
     for i in range(nx):
-        for j in range((parity + i + 1) % 2, ny - 1, 2):
+        for j in range((parity + i + i // 2 + 1) % 2, ny - 1, 2):
             a, b = i * ny + j, i * ny + j + 1
             pairs += [(a, b), (b, a)]
     return pairs

time: 29.8 us -> 28.9 us (0.970)
  the two profiles are of different devices: /device:TPU:281 before, /device:TPU:273 now
where the time goes in v6:
time: 28.9 us; the launch traced here: 28.7 us
  starting transfers between devices  10.2 us (35%)
  waiting for transfers between devices  8.13 us (28%)
  Pallas kernels  7.39 us (26%)
  blocking collectives  2.25 us (8%)
  between operations  0.69 us (2%)
    ppermute x1, waiting for transfers between devices, shards(): two = lax.ppermute(two, AXES, swap_along_gy(shape, 1))  7.35 us
    ppermute x1, starting transfers between devices, shards(): outer = lax.ppermute(outer, AXES, across)  4.29 us
    ppermute x1, starting transfers between devices, shards(): one = lax.ppermute(one, AXES, swap_along_gy(shape, 0))  3.12 us
    ppermute x1, starting transfers between devices, shards(): two = lax.ppermute(two, AXES, swap_along_gy(shape, 1))  2.81 us
    pallas_call x1, Pallas kernels, shards(): pl.pallas_call(functools.partial(last_kernel, reach), out_shape=[array(ti...  2.53 us
    pallas_call x1, Pallas kernels, shards(): pl.pallas_call(functools.partial(early_x_kernel, reach), out_shape=[field...  2.29 us
    all_gather x1, blocking collectives, shards(): inner = lax.all_gather(inner, AXES, axis_index_groups=within)  2.25 us
    pallas_call x1, Pallas kernels, shards(): pl.pallas_call(functools.partial(first_kernel, reach), out_shape=[array((...  1.67 us
  transfers between devices with their start and end apart: 3, of which 2 were waited for; matrix products, arithmetic and copies ran while one was open for 0% of the time, Pallas kernels for 10%

profile of v6, /device:TPU:273, one launch (start us, length us, event | category | flops | bytes accessed | tf_op | source)
XLA Modules:
  0.0 28.7 jit_solution(1336931060254766095)
XLA Ops:
  0.6 1.7 %weigh_blur_z.1 = (f32[24,24,128]{2,1,0:T(8,128)S(1)}, f32[22,24,128]{2,1,0:T(8,128)S(1)}, f32[22,24,128]{2,1,0:T(8,128)S(1)}, f32[68,8,128]{2,1,0:T(8,128)S(1)}...) custom-call(f32[576,128]{1,0:T(8,128)} %bitcast.13, s32[576,128]{1,0:T(8,128)} %bitcast.14, ...), custom_call_target="tpu_custom_call" | custom-call | tf_op jit(solution)/shard_map/weigh_blur_z/pallas_call | solution.py:518
  2.3 3.1 %collective-permute-start = (f32[22,24,128]{2,1,0:T(8,128)S(1)}, f32[22,24,128]{2,1,0:T(8,128)S(1)}, u32[]{:S(2)}, u32[]{:S(2)}) collective-permute-start(f32[22,24,128]{2,1,0:T(8,128)S(1)} %get-tuple-element.29), channel_id=1, source_target_pairs={{1,2},{2,1},{3,4},{4,3},{5,6},{6,5},{7,8},{8,7},{9,10},{10,9},{11,... | collective-permute-start | bytes 811016 | tf_op jit(solution)/shard_map/ppermute | solution.py:533
  5.4 2.8 %collective-permute-start.1 = (f32[22,24,128]{2,1,0:T(8,128)S(1)}, f32[22,24,128]{2,1,0:T(8,128)S(1)}, u32[]{:S(2)}, u32[]{:S(2)}) collective-permute-start(f32[22,24,128]{2,1,0:T(8,128)S(1)} %get-tuple-element.30), channel_id=1, source_target_pairs={{0,1},{1,0},{2,3},{3,2},{4,5},{5,4},{6,7},{7,6},{8,9},{9,8},{10,11... | collective-permute-start | bytes 811016 | tf_op jit(solution)/shard_map/ppermute | solution.py:534
  8.3 0.5 %own_y.1.part = f32[28,24,128]{2,1,0:T(8,128)S(1)} custom-call(f32[24,24,128]{2,1,0:T(8,128)S(1)} %get-tuple-element.27.own, f32[68,8,128]{2,1,0:T(8,128)S(1)} %get-tuple-element.28.spread), custom_call_target="tpu_custom_call" | custom-call | flops 4000000 | bytes 700000 | tf_op jit(solution)/shard_map/own_y/pallas_call | solution.py:536
  8.8 0.8 %collective-permute-done.one = f32[22,24,128]{2,1,0:T(8,128)S(1)} collective-permute-done((f32[22,24,128]{2,1,0:T(8,128)S(1)}, f32[22,24,128]{2,1,0:T(8,128)S(1)}, u32[]{:S(2)}, u32[]{:S(2)}) %collective-permute-start) | collective-permute-done | bytes 270368 | tf_op jit(solution)/shard_map/ppermute | solution.py:533
  9.5 7.4 %collective-permute-done.1.two = f32[22,24,128]{2,1,0:T(8,128)S(1)} collective-permute-done((f32[22,24,128]{2,1,0:T(8,128)S(1)}, f32[22,24,128]{2,1,0:T(8,128)S(1)}, u32[]{:S(2)}, u32[]{:S(2)}) %collective-permute-start.1) | collective-permute-done | bytes 270368 | tf_op jit(solution)/shard_map/ppermute | solution.py:534
  16.9 0.4 %rest_y.1 = (f32[768,128]{1,0:T(8,128)S(1)}, f32[604,128]{1,0:T(8,128)S(1)}, f32[604,128]{1,0:T(8,128)S(1)}) custom-call(f32[28,24,128]{2,1,0:T(8,128)S(1)} %own_y.1.part, f32[22,24,128]{2,1,0:T(8,128)S(1)} %collective-permute-done.one, f32[22,24,128]{2,1,0:T(8,128)S(1)} %collective-permute-done.1.two, s32[24,24,128]{2,1,0:T(8,128)S(1)} %bitcast.7, ...), custom_call_target="tpu_custom_call" | custom-call | tf_op jit(solution)/shard_map/rest_y/pallas_call | solution.py:548
  17.3 4.3 %collective-permute-start.2 = (f32[604,128]{1,0:T(8,128)S(1)}, f32[604,128]{1,0:T(8,128)S(1)}, u32[]{:S(2)}, u32[]{:S(2)}) collective-permute-start(f32[604,128]{1,0:T(8,128)S(1)} %get-tuple-element.49), channel_id=1, source_target_pairs={{32,64},{64,32},{33,65},{65,33},{34,66},{66,34},{35,67},{67,35},{3... | collective-permute-start | bytes 927752 | tf_op jit(solution)/shard_map/ppermute | solution.py:565
  21.6 2.3 %all-gather.1.inner = f32[2,604,128]{2,1,0:T(8,128)S(1)} all-gather(f32[1,604,128]{2,1,0:T(8,128)S(1)} %bitcast.12), channel_id=2, replica_groups={{0,32},{1,33},{2,34},{3,35},{4,36},{5,37},{6,38},{7,39},{8,40},{9,41},{..., dimensions={0}, use_global_device_ids=true | all-gather | bytes 927744 | tf_op jit(solution)/shard_map/all_gather | solution.py:566
  23.8 2.3 %early_x.1 = (f32[28,40,128]{2,1,0:T(8,128)S(1)}, f32[28,40,128]{2,1,0:T(8,128)S(1)}, f32[2,28,40,128]{3,2,1,0:T(8,128)S(1)}, f32[28,40,128]{2,1,0:T(8,128)S(1)}...) custom-call(f32[768,128]{1,0:T(8,128)S(1)} %get-tuple-element.34.blu, ...), custom_call_target="tpu_custom_call" | custom-call | flops 8000000 | bytes 3000000 | tf_op jit(solution)/shard_map/early_x/pallas_call | solution.py:570
  26.1 0.0 collective-permute-done.2.outer
  26.2 2.5 %late_x_steps.1 = (f32[24,24,128]{2,1,0:T(8,128)}, f32[2,24,24,128]{3,2,1,0:T(8,128)}) custom-call(f32[28,40,128]{2,1,0:T(8,128)S(1)} %get-tuple-element.36.part, f32[28,40,128]{2,1,0:T(8,128)S(1)} %get-tuple-element.37.coef, f32[2,28,40,128]{3,2,1,0:T(8,128)S(1)} %get-tuple-element.38.state, f32[28,40,128]{2,1,0:T(8,128)S(1)} %get-tuple-element.39.keep, ...), custom_call_target="tpu_custom_call" | custom-call | tf_op jit(solution)/shard_map/late_x_steps/pallas_call | solution.py:583
Async XLA Ops:
  2.3 7.2 %collective-permute-start = (f32[22,24,128]{2,1,0:T(8,128)S(1)}, f32[22,24,128]{2,1,0:T(8,128)S(1)}, u32[]{:S(2)}, u32[]{:S(2)}) collective-permute-start(f32[22,24,128]{2,1,0:T(8,128)S(1)} %get-tuple-element.29), channel_id=1, source_target_pairs={{1,2},{2,1},{3,4},{4,3},{5,6},{6,5},{7,8},{8,7},{9,10},{10,9},{11,... | collective-permute-start | bytes 811016 | tf_op jit(solution)/shard_map/ppermute | solution.py:533
  5.4 11.4 %collective-permute-start.1 = (f32[22,24,128]{2,1,0:T(8,128)S(1)}, f32[22,24,128]{2,1,0:T(8,128)S(1)}, u32[]{:S(2)}, u32[]{:S(2)}) collective-permute-start(f32[22,24,128]{2,1,0:T(8,128)S(1)} %get-tuple-element.30), channel_id=1, source_target_pairs={{0,1},{1,0},{2,3},{3,2},{4,5},{5,4},{6,7},{7,6},{8,9},{9,8},{10,11... | collective-permute-start | bytes 811016 | tf_op jit(solution)/shard_map/ppermute | solution.py:534
  17.3 8.9 %collective-permute-start.2 = (f32[604,128]{1,0:T(8,128)S(1)}, f32[604,128]{1,0:T(8,128)S(1)}, u32[]{:S(2)}, u32[]{:S(2)}) collective-permute-start(f32[604,128]{1,0:T(8,128)S(1)} %get-tuple-element.49), channel_id=1, source_target_pairs={{32,64},{64,32},{33,65},{65,33},{34,66},{66,34},{35,67},{67,35},{3... | collective-permute-start | bytes 927752 | tf_op jit(solution)/shard_map/ppermute | solution.py:565
